TPU v7x, 256 devices: a whole 4x4x8 slice. The times are simulated.
256 devices in a mesh: gx: 8 (over x, core), gy: 32 (over y, z).
Axes of the slice: x: 4, y: 4, z: 8, core: 2. Of those that a mesh axis runs over, the one named last changes fastest.
Arguments:
- u_electric: float32 [3, 128, 512, 128], P(None, 'gx', 'gy'), may hold values from -18 to 18
- u_magnetic: float32 [3, 128, 512, 128], P(None, 'gx', 'gy'), may hold values from -18 to 18
- eps_inv: float32 [128, 512, 128], P('gx', 'gy'), may hold values from 0.25 to 1
- metal_map: int32 [16, 64], replicated, may hold values from 0 to 1, as said below
- pole_omega: float32 [6], replicated, may hold values from 0.5 to 2
- pole_gamma: float32 [6], replicated, may hold values from 0.05 to 0.8
- pole_strength: float32 [6], replicated, may hold values from 0.3 to 1.5
Outputs:
- out_electric: float32 [3, 128, 512, 128], P(None, 'gx', 'gy')
- out_magnetic: float32 [3, 128, 512, 128], P(None, 'gx', 'gy')
- out_poles: float32 [512, 2, 6, 3, 8, 8, 128], P(('gx', 'gy'))
- coefficients: float32 [4, 3], replicated
Inputs may be any that keep to these rules, and one draw needn't show every extreme that they name: `metal_map`: each block of 2 x 2 tiles (rows 2a, 2a+1 and columns 2b, 2b+1) holds at most 2 metal tiles, and some block holds exactly 2.
All inputs are finite; a program needn't handle non-finite values.
Results may differ from a plain program's by a relative error of at most 0.0001.
Values sent between devices are 32-bit elements; how exact they have to be, the bound alone decides.
A program may use at most 192 MiB of HBM per device.

v0:
```python
import jax
import jax.numpy as jnp
from jax import lax
from jax.sharding import PartitionSpec as P

POLES = 6
STEPS = 4
MS = 2


EPSILON = 1e-06


def with_halo(cells, sides, width):
    for axis, dim in sides:
        count = lax.axis_size(axis)
        head = lax.slice_in_dim(cells, 0, width, axis=dim)
        tail = lax.slice_in_dim(cells, cells.shape[dim] - width, cells.shape[dim], axis=dim)
        cells = jnp.concatenate(
            [
                lax.ppermute(tail, axis, [(i, (i + 1) % count) for i in range(count)]),
                cells,
                lax.ppermute(head, axis, [((i + 1) % count, i) for i in range(count)]),
            ],
            axis=dim,
        )
    return cells


def pole_update(pole_state, field_tile, pole_omega, pole_gamma, pole_strength):
    polarization = pole_state[0]
    current = pole_state[1]
    summed = jnp.sum(current, axis=0)
    spring_rate = (pole_omega * pole_omega)[:, None, None, None, None]
    damping = pole_gamma[:, None, None, None, None]
    coupling = pole_strength[:, None, None, None, None]
    renewed = -spring_rate * polarization - damping * current + coupling * field_tile[None]
    return (summed, jnp.stack([current, renewed]))


def neighbour_faces(electric, magnetic):
    stacked = jnp.concatenate([electric, magnetic], axis=0)
    padded = with_halo(stacked, (("gx", 1), ("gy", 2)), 1)
    e_next_x = padded[:3, -1:, 1:-1]
    e_next_y = padded[:3, 1:-1, -1:]
    h_prev_x = padded[3:, :1, 1:-1]
    h_prev_y = padded[3:, 1:-1, :1]
    return (e_next_x, e_next_y, h_prev_x, h_prev_y)


def curls(electric, magnetic):
    e_next_x, e_next_y, h_prev_x, h_prev_y = neighbour_faces(electric, magnetic)

    def ahead_x(component):
        return (
            jnp.concatenate([electric[component, 1:], e_next_x[component]], axis=0)
            - electric[component]
        )

    def ahead_y(component):
        return (
            jnp.concatenate([electric[component, :, 1:], e_next_y[component]], axis=1)
            - electric[component]
        )

    def ahead_z(component):
        return jnp.roll(electric[component], -1, 2) - electric[component]

    def behind_x(component):
        return magnetic[component] - jnp.concatenate(
            [h_prev_x[component], magnetic[component, :-1]], axis=0
        )

    def behind_y(component):
        return magnetic[component] - jnp.concatenate(
            [h_prev_y[component], magnetic[component, :, :-1]], axis=1
        )

    def behind_z(component):
        return magnetic[component] - jnp.roll(magnetic[component], 1, 2)

    curl_e = jnp.stack([ahead_y(2) - ahead_z(1), ahead_z(0) - ahead_x(2), ahead_x(1) - ahead_y(0)])
    curl_h = jnp.stack(
        [behind_y(2) - behind_z(1), behind_z(0) - behind_x(2), behind_x(1) - behind_y(0)]
    )
    return (curl_e, curl_h)


def field_dot(first_e, first_h, second_e, second_h):
    return jnp.sum(first_e * second_e) + jnp.sum(first_h * second_h)


def body(u_electric, u_magnetic, eps_inv, metal_map, pole_omega, pole_gamma, pole_strength):
    row_index = lax.axis_index("gx")
    col_index = lax.axis_index("gy")
    half_x = u_electric.shape[1] // 2
    half_y = u_electric.shape[2] // 2
    z_depth = u_electric.shape[3]
    cell_count = (
        6.0
        * u_electric.shape[1]
        * u_electric.shape[2]
        * z_depth
        * lax.axis_size("gx")
        * lax.axis_size("gy")
    )
    own_tiles = lax.dynamic_slice(metal_map, (2 * row_index, 2 * col_index), (2, 2)).reshape(4)
    before = jnp.cumsum(own_tiles) - own_tiles
    tile_order = jnp.arange(4, dtype=jnp.int32)
    corners = []
    present = []
    for slot_id in range(MS):
        picked = jnp.logical_and(own_tiles == 1, before == slot_id).astype(jnp.int32)
        tile_number = jnp.sum(picked * tile_order)
        present.append(jnp.sum(picked) > 0)
        corners.append((tile_number // 2 * half_x, tile_number % 2 * half_y))
    last_slot = MS - 1
    handed = jnp.zeros((), jnp.bool_)
    tile_shape = (3, half_x, half_y, z_depth)
    scale_u = (
        lax.psum(field_dot(u_electric, u_magnetic, u_electric, u_magnetic), ("gx", "gy"))
        / cell_count
    )
    root_value = jnp.sqrt(scale_u + EPSILON)
    q_e = u_electric / root_value
    q_h = u_magnetic / root_value
    v_e, v_h = (q_e, q_h)
    v_poles = jnp.zeros((MS, 2, POLES, 3, half_x, half_y, z_depth), jnp.float32)
    coeff_rows = []
    for step_id in range(STEPS):
        curl_e, curl_h = curls(v_e, v_h)
        summed_list = []
        renewed_list = []
        for apply_slot_id in range(MS):
            apply_active = present[apply_slot_id]
            if apply_slot_id == last_slot:
                apply_active = jnp.logical_and(apply_active, jnp.logical_not(handed))
            corner = corners[apply_slot_id]
            pole_state = v_poles[apply_slot_id]
            field_tile = lax.dynamic_slice(v_e, (0, corner[0], corner[1], 0), tile_shape)
            summed, renewed = lax.cond(
                apply_active,
                lambda: pole_update(pole_state, field_tile, pole_omega, pole_gamma, pole_strength),
                lambda: (jnp.zeros_like(field_tile), jnp.zeros_like(pole_state)),
            )
            summed_list.append(summed)
            renewed_list.append(renewed)
        pole_term = jnp.zeros_like(v_e)
        for apply_slot_id in range(MS):
            start_index = (0, corners[apply_slot_id][0], corners[apply_slot_id][1], 0)
            existing = lax.dynamic_slice(pole_term, start_index, tile_shape)
            pole_term = lax.dynamic_update_slice(
                pole_term, existing + summed_list[apply_slot_id], start_index
            )
        w_e = eps_inv[None] * (curl_h - pole_term)
        w_h = -curl_e
        w_poles = jnp.stack(renewed_list)
        along_q, along_v = lax.psum(
            (field_dot(q_e, q_h, w_e, w_h), field_dot(v_e, v_h, w_e, w_h)), ("gx", "gy")
        )
        along_q = along_q / cell_count
        along_v = along_v / cell_count
        if step_id == 0:
            along_v = jnp.zeros_like(along_v)
        z_e = w_e - along_q * q_e - along_v * v_e
        z_h = w_h - along_q * q_h - along_v * v_h
        squared = lax.psum(field_dot(z_e, z_h, z_e, z_h), ("gx", "gy")) / cell_count
        norm_value = jnp.sqrt(squared + EPSILON)
        v_e = z_e / norm_value
        v_h = z_h / norm_value
        v_poles = (w_poles - along_v * v_poles) / norm_value
        coeff_rows.append(jnp.stack([along_q, along_v, norm_value]))
    return (v_e, v_h, v_poles, jnp.stack(coeff_rows))


def solution(mesh):
    placed = (
        P(None, "gx", "gy", None),
        P(None, "gx", "gy", None),
        P("gx", "gy", None),
        P(),
        P(),
        P(),
        P(),
    )
    return jax.shard_map(
        body,
        mesh=mesh,
        in_specs=placed,
        out_specs=(
            P(None, "gx", "gy", None),
            P(None, "gx", "gy", None),
            P(("gx", "gy"), None, None, None, None, None, None),
            P(),
        ),
        check_vma=False,
    )
```

profile of v0, /device:TPU:1, one launch (start us, length us, event | category | flops | bytes accessed | tf_op | source)
XLA Modules:
  0.0 872.0 jit_solution(17271546913225244516)
XLA Ops:
  0.6 1.8 multiply_reduce_fusion.22
  3.8 81.4 %psum.84 = f32[]{:T(128)} all-reduce(f32[]{:T(128)S(6)} %add.246), channel_id=1, replica_groups=mesh['gx'=8,'gy'=32] {'gx','gy'}, use_global_device_ids=true, to_apply=%region_2.3 | all-reduce | flops 1 | bytes 8 | tf_op jit(solution)/shard_map/psum | solution.py:121
  110.4 1.6 add_dynamic-update-slice_fusion.3
  112.9 1.1 collective-permute-start.3
  114.0 3.8 collective-permute-start.2
  119.2 1.4 fusion.19
  123.7 76.8 %psum.85 = f32[]{:T(128)} all-reduce(f32[]{:T(128)S(6)} %add.257), channel_id=1, replica_groups=mesh['gx'=8,'gy'=32] {'gx','gy'}, use_global_device_ids=true, to_apply=%region_14.15 | all-reduce | flops 1 | bytes 8 | tf_op jit(solution)/shard_map/psum | solution.py:158
  201.2 1.7 multiply_reduce_fusion.18
  204.9 72.3 %psum.86 = f32[]{:T(128)} all-reduce(f32[]{:T(128)S(6)} %add.258), channel_id=1, replica_groups=mesh['gx'=8,'gy'=32] {'gx','gy'}, use_global_device_ids=true, to_apply=%region_17.18 | all-reduce | flops 1 | bytes 8 | tf_op jit(solution)/shard_map/psum | solution.py:167
  277.9 1.1 broadcast_divide_fusion.6
  279.1 1.8 maximum_divide_fusion
  290.9 1.1 collective-permute-start.4
  293.2 1.2 conditional.10
  293.2 1.1 stack.171
  297.1 1.2 pad_maximum_fusion.8
  298.3 7.1 collective-permute-start.6
  305.3 1.6 collective-permute-start.7
  308.6 1.5 fusion.28
  311.2 1.5 multiply_reduce_fusion.17
  315.1 76.7 %all-reduce.4 = (f32[]{:T(128)}, f32[]{:T(128)}) all-reduce(f32[]{:T(128)S(6)} %add.262, f32[]{:T(128)S(6)} %add.261), channel_id=1, replica_groups=mesh['gx'=8,'gy'=32] {'gx','gy'}, use_global_device_ids=true, to_apply=%region_29.30 | all-reduce | flops 2 | bytes 16 | tf_op jit(solution)/shard_map/psum | solution.py:158
  393.1 2.8 multiply_reduce_fusion.12
  396.0 2.4 multiply_reduce_fusion.13
  399.7 73.0 %psum.89 = f32[]{:T(128)} all-reduce(f32[]{:T(128)S(6)} %add.263), channel_id=1, replica_groups=mesh['gx'=8,'gy'=32] {'gx','gy'}, use_global_device_ids=true, to_apply=%region_32.33 | all-reduce | flops 1 | bytes 8 | tf_op jit(solution)/shard_map/psum | solution.py:167
  474.5 2.2 fusion.12
  486.9 1.1 collective-permute-start.8
  492.1 1.2 pad_maximum_fusion.7
  493.3 4.7 collective-permute-start.11
  498.0 1.8 collective-permute-start.10
  501.3 1.5 fusion.31
  503.9 1.5 multiply_reduce_fusion.11
  507.9 79.1 %all-reduce.3 = (f32[]{:T(128)}, f32[]{:T(128)}) all-reduce(f32[]{:T(128)S(6)} %add.267, f32[]{:T(128)S(6)} %add.266), channel_id=1, replica_groups=mesh['gx'=8,'gy'=32] {'gx','gy'}, use_global_device_ids=true, to_apply=%region_44.45 | all-reduce | flops 2 | bytes 16 | tf_op jit(solution)/shard_map/psum | solution.py:158
  588.2 2.7 multiply_reduce_fusion.6
  590.9 2.5 multiply_reduce_fusion.7
  594.7 72.3 %psum.92 = f32[]{:T(128)} all-reduce(f32[]{:T(128)S(6)} %add.268), channel_id=1, replica_groups=mesh['gx'=8,'gy'=32] {'gx','gy'}, use_global_device_ids=true, to_apply=%region_47.48 | all-reduce | flops 1 | bytes 8 | tf_op jit(solution)/shard_map/psum | solution.py:167
  668.8 3.9 fusion.13
  682.7 1.1 collective-permute-start.12
  686.0 2.1 add_dynamic-update-slice_fusion
  688.2 1.2 pad_maximum_fusion
  689.4 7.0 collective-permute-start.14
  696.4 1.6 collective-permute-start.15
  699.7 1.5 fusion.40
  702.3 1.5 multiply_reduce_fusion.5
  706.6 76.3 %all-reduce.2 = (f32[]{:T(128)}, f32[]{:T(128)}) all-reduce(f32[]{:T(128)S(6)} %add.272, f32[]{:T(128)S(6)} %add.271), channel_id=1, replica_groups=mesh['gx'=8,'gy'=32] {'gx','gy'}, use_global_device_ids=true, to_apply=%region_59.60 | all-reduce | flops 2 | bytes 16 | tf_op jit(solution)/shard_map/psum | solution.py:158
  784.2 2.8 multiply_reduce_fusion
  787.0 2.5 multiply_reduce_fusion.1
  790.9 72.8 %psum.95 = f32[]{:T(128)} all-reduce(f32[]{:T(128)S(6)} %add.273), channel_id=1, replica_groups=mesh['gx'=8,'gy'=32] {'gx','gy'}, use_global_device_ids=true, to_apply=%region_62.63 | all-reduce | flops 1 | bytes 8 | tf_op jit(solution)/shard_map/psum | solution.py:167
  864.4 1.9 broadcast_divide_fusion.1
  867.1 4.3 fusion.14
  (343 shorter events, 76.0 us)
Async XLA Ops:
  87.9 24.1 %copy-start.5 = (f32[3,16,16,128]{3,2,1,0:T(8,128)}, f32[3,16,16,128]{3,2,1,0:T(8,128)S(1)}, u32[]{:S(2)}) copy-start(f32[3,16,16,128]{3,2,1,0:T(8,128)S(1)} %broadcast_divide_fusion.8) | copy-start | bytes 1179652
  88.6 23.4 %collective-permute-start.1 = (f32[6,1,16,128]{3,2,1,0:T(8,128)}, f32[6,1,16,128]{3,2,1,0:T(8,128)}, u32[]{:S(2)}, u32[]{:S(2)}) collective-permute-start(f32[6,1,16,128]{3,2,1,0:T(8,128)} %get-tuple-element.601), channel_id=1, source_target_pairs={{32,0},{64,32},{96,64},{128,96},{160,128},{192,160},{224,192},{0,2... | collective-permute-start | bytes 147464 | tf_op jit(solution)/shard_map/ppermute | solution.py:23
  89.5 22.5 %collective-permute-start = (f32[6,1,16,128]{3,2,1,0:T(8,128)}, f32[6,1,16,128]{3,2,1,0:T(8,128)}, u32[]{:S(2)}, u32[]{:S(2)}) collective-permute-start(f32[6,1,16,128]{3,2,1,0:T(8,128)} %get-tuple-element.602), channel_id=1, source_target_pairs={{0,32},{32,64},{64,96},{96,128},{128,160},{160,192},{192,224},{224... | collective-permute-start | bytes 147464 | tf_op jit(solution)/shard_map/ppermute | solution.py:21
  112.9 8.5 collective-permute-start.3
  114.0 5.2 collective-permute-start.2
  122.5 155.4 %copy-start.34 = (f32[3,16,16,128]{3,2,1,0:T(8,128)}, f32[3,16,16,128]{3,2,1,0:T(8,128)S(1)}, u32[]{:S(2)}) copy-start(f32[3,16,16,128]{3,2,1,0:T(8,128)S(1)} %get-tuple-element.574) | copy-start | bytes 1179652
  290.2 6.8 collective-permute-start.5
  290.9 6.2 collective-permute-start.4
  294.4 15.7 %copy-start.25 = (f32[1,16,16,128]{3,2,1,0:T(8,128)S(1)}, f32[1,16,16,128]{3,2,1,0:T(8,128)}, u32[]{:S(2)}) copy-start(f32[1,16,16,128]{3,2,1,0:T(8,128)} %copy-done.23) | copy-start | bytes 393220
  294.4 15.8 %copy-start.28 = (f32[1,16,16,128]{3,2,1,0:T(8,128)S(1)}, f32[1,16,16,128]{3,2,1,0:T(8,128)}, u32[]{:S(2)}) copy-start(f32[1,16,16,128]{3,2,1,0:T(8,128)} %copy-done.26) | copy-start | bytes 393220
  294.4 15.8 %copy-start.31 = (f32[1,16,16,128]{3,2,1,0:T(8,128)S(1)}, f32[1,16,16,128]{3,2,1,0:T(8,128)}, u32[]{:S(2)}) copy-start(f32[1,16,16,128]{3,2,1,0:T(8,128)} %copy-done.29) | copy-start | bytes 393220
  295.0 15.9 %copy-start.12 = (f32[3,16,16,128]{3,2,1,0:T(8,128)S(1)}, f32[3,16,16,128]{3,2,1,0:T(8,128)}, u32[]{:S(2)}) copy-start(f32[3,16,16,128]{3,2,1,0:T(8,128)} %copy-done.11) | copy-start | bytes 1179652
  295.1 15.9 %copy-start.63 = (f32[1,16,16,127]{3,2,1,0:T(8,128)S(1)}, f32[1,16,16,127]{3,2,1,0:T(8,128)}, u32[]{:S(2)}) copy-start(f32[1,16,16,127]{3,2,1,0:T(8,128)} %slice_bitcast_fusion.28) | copy-start | bytes 390148
  295.1 15.9 %copy-start.64 = (f32[1,16,16,1]{3,2,1,0:T(8,128)S(1)}, f32[1,16,16,1]{3,2,1,0:T(8,128)}, u32[]{:S(2)}) copy-start(f32[1,16,16,1]{3,2,1,0:T(8,128)} %slice_bitcast_fusion.29) | copy-start | bytes 3076
  295.1 15.9 %copy-start.67 = (f32[1,16,16,127]{3,2,1,0:T(8,128)S(1)}, f32[1,16,16,127]{3,2,1,0:T(8,128)}, u32[]{:S(2)}) copy-start(f32[1,16,16,127]{3,2,1,0:T(8,128)} %slice_bitcast_fusion.26) | copy-start | bytes 390148
  295.1 15.9 %copy-start.68 = (f32[1,16,16,1]{3,2,1,0:T(8,128)S(1)}, f32[1,16,16,1]{3,2,1,0:T(8,128)}, u32[]{:S(2)}) copy-start(f32[1,16,16,1]{3,2,1,0:T(8,128)} %slice_bitcast_fusion.27) | copy-start | bytes 3076
  295.1 15.9 %copy-start.75 = (f32[1,16,15,128]{3,2,1,0:T(8,128)S(1)}, f32[1,16,15,128]{3,2,1,0:T(8,128)}, u32[]{:S(2)}) copy-start(f32[1,16,15,128]{3,2,1,0:T(8,128)} %get-tuple-element.653) | copy-start | bytes 368644
  295.1 15.9 %copy-start.76 = (f32[1,16,15,128]{3,2,1,0:T(8,128)S(1)}, f32[1,16,15,128]{3,2,1,0:T(8,128)}, u32[]{:S(2)}) copy-start(f32[1,16,15,128]{3,2,1,0:T(8,128)} %get-tuple-element.654) | copy-start | bytes 368644
  295.1 15.9 %copy-start.83 = (f32[1,15,16,128]{3,2,1,0:T(8,128)S(1)}, f32[1,15,16,128]{3,2,1,0:T(8,128)}, u32[]{:S(2)}) copy-start(f32[1,15,16,128]{3,2,1,0:T(8,128)} %get-tuple-element.655) | copy-start | bytes 368644
  295.1 15.9 %copy-start.84 = (f32[1,15,16,128]{3,2,1,0:T(8,128)S(1)}, f32[1,15,16,128]{3,2,1,0:T(8,128)}, u32[]{:S(2)}) copy-start(f32[1,15,16,128]{3,2,1,0:T(8,128)} %get-tuple-element.656) | copy-start | bytes 368644
  298.3 12.7 %collective-permute-start.6 = (f32[6,18,1,128]{3,2,1,0:T(1,128)S(1)}, f32[6,18,1,128]{3,2,1,0:T(1,128)S(1)}, u32[]{:S(2)}, u32[]{:S(2)}) collective-permute-start(f32[6,18,1,128]{3,2,1,0:T(1,128)S(1)} %get-tuple-element.592), channel_id=1, source_target_pairs={{0,1},{1,2},{2,3},{3,4},{4,5},{5,6},{6,7},{7,8},{8,9},{9,10},{10,1... | collective-permute-start | bytes 165896 | tf_op jit(solution)/shard_map/ppermute | solution.py:21
  305.3 3.3 collective-permute-start.7
  486.3 5.8 collective-permute-start.9
  486.9 5.2 collective-permute-start.8
  489.4 14.2 %copy-start.14 = (f32[1,2,6,3,8,8,128]{6,5,4,3,2,1,0:T(8,128)}, f32[1,2,6,3,8,8,128]{6,5,4,3,2,1,0:T(8,128)S(1)}, u32[]{:S(2)}) copy-start(f32[1,2,6,3,8,8,128]{6,5,4,3,2,1,0:T(8,128)S(1)} %get-tuple-element.318) | copy-start | bytes 3538948
  490.1 13.5 %copy-start.10 = (f32[3,16,16,128]{3,2,1,0:T(8,128)S(1)}, f32[3,16,16,128]{3,2,1,0:T(8,128)}, u32[]{:S(2)}) copy-start(f32[3,16,16,128]{3,2,1,0:T(8,128)} %copy-done.9) | copy-start | bytes 1179652
  490.1 13.5 %copy-start.61 = (f32[1,16,16,127]{3,2,1,0:T(8,128)S(1)}, f32[1,16,16,127]{3,2,1,0:T(8,128)}, u32[]{:S(2)}) copy-start(f32[1,16,16,127]{3,2,1,0:T(8,128)} %slice_bitcast_fusion.16) | copy-start | bytes 390148
  490.1 13.5 %copy-start.62 = (f32[1,16,16,1]{3,2,1,0:T(8,128)S(1)}, f32[1,16,16,1]{3,2,1,0:T(8,128)}, u32[]{:S(2)}) copy-start(f32[1,16,16,1]{3,2,1,0:T(8,128)} %slice_bitcast_fusion.17) | copy-start | bytes 3076
  493.3 10.3 %collective-permute-start.11 = (f32[6,18,1,128]{3,2,1,0:T(1,128)S(1)}, f32[6,18,1,128]{3,2,1,0:T(1,128)S(1)}, u32[]{:S(2)}, u32[]{:S(2)}) collective-permute-start(f32[6,18,1,128]{3,2,1,0:T(1,128)S(1)} %get-tuple-element.590), channel_id=1, source_target_pairs={{0,1},{1,2},{2,3},{3,4},{4,5},{5,6},{6,7},{7,8},{8,9},{9,10},{10,1... | collective-permute-start | bytes 165896 | tf_op jit(solution)/shard_map/ppermute | solution.py:21
  498.0 3.2 collective-permute-start.10
  503.7 87.3 %copy-start.18 = (f32[3,16,16,128]{3,2,1,0:T(8,128)S(1)}, f32[3,16,16,128]{3,2,1,0:T(8,128)}, u32[]{:S(2)}) copy-start(f32[3,16,16,128]{3,2,1,0:T(8,128)} %get-tuple-element.571) | copy-start | bytes 1179652
  682.0 6.1 collective-permute-start.13
  682.7 5.5 collective-permute-start.12
  685.9 16.4 %copy-start.33 = (f32[1,2,6,3,8,8,128]{6,5,4,3,2,1,0:T(8,128)}, f32[1,2,6,3,8,8,128]{6,5,4,3,2,1,0:T(8,128)S(1)}, u32[]{:S(2)}) copy-start(f32[1,2,6,3,8,8,128]{6,5,4,3,2,1,0:T(8,128)S(1)} %get-tuple-element.323) | copy-start | bytes 3538948
  685.9 15.3 %copy-start.20 = (f32[3,16,16,128]{3,2,1,0:T(8,128)S(1)}, f32[3,16,16,128]{3,2,1,0:T(8,128)}, u32[]{:S(2)}) copy-start(f32[3,16,16,128]{3,2,1,0:T(8,128)} %get-tuple-element.564) | copy-start | bytes 1179652
  686.0 16.1 %copy-start.8 = (f32[3,16,16,128]{3,2,1,0:T(8,128)S(1)}, f32[3,16,16,128]{3,2,1,0:T(8,128)}, u32[]{:S(2)}) copy-start(f32[3,16,16,128]{3,2,1,0:T(8,128)} %copy-done.7) | copy-start | bytes 1179652
  686.0 16.1 %copy-start.57 = (f32[1,16,16,127]{3,2,1,0:T(8,128)S(1)}, f32[1,16,16,127]{3,2,1,0:T(8,128)}, u32[]{:S(2)}) copy-start(f32[1,16,16,127]{3,2,1,0:T(8,128)} %slice_bitcast_fusion.12) | copy-start | bytes 390148
  686.0 16.1 %copy-start.58 = (f32[1,16,16,1]{3,2,1,0:T(8,128)S(1)}, f32[1,16,16,1]{3,2,1,0:T(8,128)}, u32[]{:S(2)}) copy-start(f32[1,16,16,1]{3,2,1,0:T(8,128)} %slice_bitcast_fusion.13) | copy-start | bytes 3076
  686.0 16.1 %copy-start.59 = (f32[1,16,16,127]{3,2,1,0:T(8,128)S(1)}, f32[1,16,16,127]{3,2,1,0:T(8,128)}, u32[]{:S(2)}) copy-start(f32[1,16,16,127]{3,2,1,0:T(8,128)} %slice_bitcast_fusion.10) | copy-start | bytes 390148
  686.0 16.1 %copy-start.60 = (f32[1,16,16,1]{3,2,1,0:T(8,128)S(1)}, f32[1,16,16,1]{3,2,1,0:T(8,128)}, u32[]{:S(2)}) copy-start(f32[1,16,16,1]{3,2,1,0:T(8,128)} %slice_bitcast_fusion.11) | copy-start | bytes 3076
  686.0 16.1 %copy-start.71 = (f32[1,16,15,128]{3,2,1,0:T(8,128)S(1)}, f32[1,16,15,128]{3,2,1,0:T(8,128)}, u32[]{:S(2)}) copy-start(f32[1,16,15,128]{3,2,1,0:T(8,128)} %get-tuple-element.617) | copy-start | bytes 368644
  686.0 16.1 %copy-start.72 = (f32[1,16,15,128]{3,2,1,0:T(8,128)S(1)}, f32[1,16,15,128]{3,2,1,0:T(8,128)}, u32[]{:S(2)}) copy-start(f32[1,16,15,128]{3,2,1,0:T(8,128)} %get-tuple-element.618) | copy-start | bytes 368644
  686.0 16.1 %copy-start.79 = (f32[1,15,16,128]{3,2,1,0:T(8,128)S(1)}, f32[1,15,16,128]{3,2,1,0:T(8,128)}, u32[]{:S(2)}) copy-start(f32[1,15,16,128]{3,2,1,0:T(8,128)} %get-tuple-element.619) | copy-start | bytes 368644
  686.0 16.1 %copy-start.80 = (f32[1,15,16,128]{3,2,1,0:T(8,128)S(1)}, f32[1,15,16,128]{3,2,1,0:T(8,128)}, u32[]{:S(2)}) copy-start(f32[1,15,16,128]{3,2,1,0:T(8,128)} %get-tuple-element.620) | copy-start | bytes 368644
  689.4 12.6 %collective-permute-start.14 = (f32[6,18,1,128]{3,2,1,0:T(1,128)S(1)}, f32[6,18,1,128]{3,2,1,0:T(1,128)S(1)}, u32[]{:S(2)}, u32[]{:S(2)}) collective-permute-start(f32[6,18,1,128]{3,2,1,0:T(1,128)S(1)} %get-tuple-element.588), channel_id=1, source_target_pairs={{0,1},{1,2},{2,3},{3,4},{4,5},{5,6},{6,7},{7,8},{8,9},{9,10},{10,1... | collective-permute-start | bytes 165896 | tf_op jit(solution)/shard_map/ppermute | solution.py:21
  696.4 3.3 collective-permute-start.15
  702.1 84.9 %copy-start.16 = (f32[3,16,16,128]{3,2,1,0:T(8,128)S(1)}, f32[3,16,16,128]{3,2,1,0:T(8,128)}, u32[]{:S(2)}) copy-start(f32[3,16,16,128]{3,2,1,0:T(8,128)} %get-tuple-element.566) | copy-start | bytes 1179652
  787.0 79.3 %copy-start.43 = (f32[3,16,16,128]{3,2,1,0:T(8,128)S(1)}, f32[3,16,16,128]{3,2,1,0:T(8,128)}, u32[]{:S(2)}) copy-start(f32[3,16,16,128]{3,2,1,0:T(8,128)} %get-tuple-element.559) | copy-start | bytes 1179652
  (60 other events, 351.6 us)
where the time goes:
time: 875 us; the launch traced here: 872 us
  blocking collectives  681 us (78%)
  other arithmetic  70.9 us (8%)
  local copies, waits for them, and re-layouts  52.3 us (6%)
  starting transfers between devices  35.6 us (4%)
  between operations  31.9 us (4%)
    psum x4, blocking collectives, body(): lax.psum((field_dot(q_e, q_h, w_e, w_h), field_dot(v_e, v_h, w_e, w_h)),...  309 us
    psum x4, blocking collectives, body(): squared = lax.psum(field_dot(z_e, z_h, z_e, z_h), ('gx', 'gy')) / cell_count  290 us
    psum x1, blocking collectives, body(): lax.psum(field_dot(u_electric, u_magnetic, u_electric, u_magnetic), ('gx'...  81.4 us
    reduce_sum x17, other arithmetic, field_dot(): return jnp.sum(first_e * second_e) + jnp.sum(first_h * second_h)  28.2 us
    ppermute x8, starting transfers between devices, with_halo(): lax.ppermute(tail, axis, [(i, (i + 1) % count) for i in range(count)])  23.9 us
  transfers between devices with their start and end apart: 16, of which 2 were waited for; matrix products, arithmetic and copies ran while one was open for 4% of the time, Pallas kernels for 0%

commit v1 on v0

v1 whole, which is shorter than its diff:
```python
import functools

import jax
import jax.numpy as jnp
from jax import lax
from jax.experimental import pallas as pl
from jax.experimental.pallas import tpu as pltpu
from jax.sharding import PartitionSpec as P

POLES = 6
STEPS = 4
MS = 2
EPSILON = 1e-06
MESH = pl.DeviceIdType.MESH

EDGE = 2
OWN = 16
PADX = OWN + 2 * EDGE
PADY = 24
HIGH = 16
LOW = 22
FIELDS = 7
TO_PREVIOUS = [(f, 0) for f in range(FIELDS)] + [(f, 1) for f in (0, 2, 3, 4, 5, 6)]
TO_NEXT = [(f, 1) for f in range(FIELDS)] + [(f, 0) for f in (0, 1, 2, 3, 5)]
ROW = PADX * PADY
CORNER_ROWS = 32
PAIRS = [(i, j) for i in range(STEPS + 1) for j in range(i, STEPS + 1)]
VMEM_LIMIT = 40 * 1024 * 1024


def layout(gx_size, gy_size):
    cores = 2
    z_size = min(8, gy_size // 2)
    return gx_size // cores, cores, gy_size // z_size, z_size


def rings(sizes):
    result = []
    for axis, size in (("x", sizes[0]), ("y", sizes[2]), ("z", sizes[3])):
        near = sorted({1 % size, size - 1} - {0})
        far = sorted({2 % size, (size - 2) % size} - {0}) if size > 3 else []
        result.append((axis, size, near, far))
    return result


def farthest_first(first, second):
    def hops(step, size):
        return min(step, size - step)

    steps = [(a, b) for a in range(first) for b in range(second) if a or b]
    return sorted(steps, key=lambda step: -hops(step[0], first) - hops(step[1], second))


def next_y(value):
    return pltpu.roll(value, PADY - 1, 0)


def prev_y(value):
    return pltpu.roll(value, 1, 0)


def next_z(value):
    return pltpu.roll(value, value.shape[1] - 1, 1)


def prev_z(value):
    return pltpu.roll(value, 1, 1)


def settle(buffer, semaphore):
    pltpu.make_async_copy(buffer, buffer, semaphore).wait()


def exchange_kernel(
    sizes,
    tiles,
    u_e,
    u_h,
    eps_in,
    metal_in,
    omega_in,
    gamma_in,
    strength_in,
    k1,
    k2,
    k3,
    k4,
    gram_out,
    tiles_out,
    kicks_out,
    raw,
    face_in,
    u,
    previous_out,
    previous_in,
    next_out,
    next_in,
    corner_out,
    corner_in,
    mask,
    acc_rows,
    sum_a,
    sum_b,
    metal,
    omega,
    gamma,
    strength,
    heard,
    load_sem,
    face_send,
    face_recv,
    stage_send,
    stage_recv,
):
    x_size, cores, y_size, z_size = sizes
    gx_size, gy_size = x_size * cores, y_size * z_size
    gx = lax.axis_index("gx")
    gy = lax.axis_index("gy")

    loads = [
        pltpu.make_async_copy(u_e, raw.at[pl.ds(0, 3)], load_sem.at[0]),
        pltpu.make_async_copy(u_h, raw.at[pl.ds(3, 3)], load_sem.at[1]),
        pltpu.make_async_copy(eps_in, raw.at[6], load_sem.at[2]),
        pltpu.make_async_copy(metal_in, metal, load_sem.at[3]),
        pltpu.make_async_copy(omega_in, omega, load_sem.at[4]),
        pltpu.make_async_copy(gamma_in, gamma, load_sem.at[5]),
        pltpu.make_async_copy(strength_in, strength, load_sem.at[6]),
    ]
    for load in loads:
        load.start()

    def ring(position, size):
        return [position] + [lax.rem(position + step, size) for step in range(1, size)]

    def device(x, core, y, z):
        return (x * cores + core, y * z_size + z)

    around_x = {0: gx, -1: lax.rem(gx + gx_size - 1, gx_size), 1: lax.rem(gx + 1, gx_size)}
    around_y = {0: gy, -1: lax.rem(gy + gy_size - 1, gy_size), 1: lax.rem(gy + 1, gy_size)}

    def neighbour(dx, dy):
        return (around_x[dx], around_y[dy])

    my_x, my_core = lax.div(gx, cores), lax.rem(gx, cores)
    my_y, my_z = lax.div(gy, z_size), lax.rem(gy, z_size)
    ring_x, ring_core = ring(my_x, x_size), ring(my_core, cores)
    ring_y, ring_z = ring(my_y, y_size), ring(my_z, z_size)

    def along(axis, step, core=0):
        return device(
            ring_x[step if axis == "x" else 0],
            ring_core[core],
            ring_y[step if axis == "y" else 0],
            ring_z[step if axis == "z" else 0],
        )

    def signal(semaphore, target):
        pl.semaphore_signal(semaphore, inc=1, device_id=target, device_id_type=MESH)

    beside = [(0, -1), (0, 1), (-1, 0), (1, 0)]
    near = [(axis, step, 0) for axis, _, steps, _ in rings(sizes) for step in steps]
    near += [(axis, step, 1) for axis, step, _ in near if axis == "z"]
    far = [(axis, step) for axis, _, _, steps in rings(sizes) for step in steps]
    barrier = pltpu.get_barrier_semaphore()
    for dx, dy in beside:
        signal(barrier, neighbour(dx, dy))
    for place in near:
        signal(barrier, along(*place))

    for load in loads:
        load.wait()

    for number, (f, layer) in enumerate(TO_PREVIOUS):
        previous_out[number] = raw[f, pl.ds(layer, OWN, stride=OWN), :]
    for number, (f, layer) in enumerate(TO_NEXT):
        next_out[number] = raw[f, pl.ds(OWN - 2 + layer, OWN, stride=OWN), :]
    corners = [(0, 0), (0, 1), (1, 0), (1, 1)]
    for number, (side_x, side_y) in enumerate(corners):
        for f in range(FIELDS):
            for layer in range(2):
                if side_x != side_y:
                    x = (0 if side_x == 0 else OWN - 2) + layer
                    y = 0 if side_y == 0 else OWN - 2
                    cells = raw[f, pl.ds(x * OWN + y, 2), :]
                    corner_out[number, pl.ds(f * 4 + layer * 2, 2), :] = cells
                elif layer == 0:
                    cell = 0 if side_x == 0 else OWN * OWN - 1
                    corner_out[number, pl.ds(f, 1), :] = raw[f, pl.ds(cell, 1), :]

    pl.semaphore_wait(barrier, len(beside) + len(near))

    copies = []

    def send(src, dst, device):
        number = len(copies)
        copy = pltpu.make_async_remote_copy(
            src_ref=src,
            dst_ref=dst,
            send_sem=face_send.at[number],
            recv_sem=face_recv.at[number],
            device_id=device,
            device_id_type=MESH,
        )
        copy.start()
        copies.append(copy)

    send(previous_out, previous_in, neighbour(0, -1))
    send(next_out, next_in, neighbour(0, 1))
    everything = pl.ds(0, FIELDS)
    layers = EDGE * OWN
    send(raw.at[everything, pl.ds(0, layers)], face_in.at[0], neighbour(-1, 0))
    send(raw.at[everything, pl.ds(OWN * OWN - layers, layers)], face_in.at[1], neighbour(1, 0))
    for dx, dy in beside[2:]:
        signal(heard.at[0], neighbour(dx, dy))
    for place in near:
        signal(heard.at[0], along(*place))

    tile_rows = [lax.rem(2 * gx + s - 1 + tiles[0], tiles[0]) for s in range(4)]
    tile_cols = [lax.rem(2 * gy + t - 1 + tiles[1], tiles[1]) for t in range(4)]
    upper = lax.broadcasted_iota(jnp.int32, (8, 128), 0) < 4
    for s in range(4):
        flag = [
            jnp.full((8, 128), metal[tile_rows[s], tile_cols[t]].astype(jnp.float32)) for t in range(4)
        ]
        mask[s, 0:8] = flag[1]
        mask[s, 8:16] = flag[2]
        mask[s, 16:24] = jnp.where(upper, flag[3], flag[0])

    response = [jnp.float32(0.0)] * 3
    for p in range(POLES):
        g0 = strength[p]
        g1 = -gamma[p] * g0
        g2 = -(omega[p] * omega[p]) * g0 - gamma[p] * g1
        response = [response[0] + g0, response[1] + g1, response[2] + g2]

    def copy_own(x, carry):
        for f in range(FIELDS):
            source = raw[f, pl.ds(pl.multiple_of(x * OWN, 8), OWN), :]
            u[f, pl.ds(pl.multiple_of((x + EDGE) * PADY, 8), OWN), :] = source
        return carry

    lax.fori_loop(0, OWN, copy_own, 0)

    pl.semaphore_wait(heard.at[0], len(beside[2:]) + len(near))
    for axis, step in far:
        signal(heard.at[1], along(axis, step))
    for number, (side_x, side_y) in enumerate(corners):
        rows = pl.ds(0, 8 if side_x == side_y else CORNER_ROWS)
        send(
            corner_out.at[number, rows],
            corner_in.at[number, rows],
            neighbour(2 * side_x - 1, 2 * side_y - 1),
        )

    class Padded:
        def __getitem__(self, at):
            f, x = at
            return u[f, pl.ds(pl.multiple_of(x * PADY, 8), PADY), :]

    start = Padded()
    states = [start, k1, k2, k3, k4]

    def electric(step, x):
        old = states[step - 1]
        hx, hy, hz = old[3, x], old[4, x], old[5, x]
        hy_back, hz_back = old[4, x - 1], old[5, x - 1]
        curl = [
            (hz - prev_y(hz)) - (hy - prev_z(hy)),
            (hx - prev_z(hx)) - (hz - hz_back),
            (hy - hy_back) - (hx - prev_y(hx)),
        ]
        eps = start[6, x]
        if step > 1:
            metal_here = mask[(x + 6) // 8]
            for c in range(3):
                current = response[step - 2] * start[c, x]
                for j in range(1, step - 1):
                    current = current + response[step - 2 - j] * states[j][c, x]
                curl[c] = curl[c] - metal_here * current
        return [eps * part for part in curl]

    def magnetic(step, x):
        old = states[step - 1]
        ex, ey, ez = old[0, x], old[1, x], old[2, x]
        ey_next, ez_next = old[1, x + 1], old[2, x + 1]
        return [
            (next_z(ey) - ey) - (next_y(ez) - ez),
            (ez_next - ez) - (next_z(ex) - ex),
            (next_y(ex) - ex) - (ey_next - ey),
        ]

    def write_rows(step, starts, shift):
        new = states[step]
        parts = [(x, electric(step, x), magnetic(step, x - shift)) for x in starts]
        for x, of_e, of_h in parts:
            for c in range(3):
                new[c, x] = of_e[c]
                new[3 + c, x - shift] = of_h[c]

    def interior(step, low, high, shift):
        def rows(x, carry):
            write_rows(step, [x], shift)
            return carry

        lax.fori_loop(low, high, rows, 0)

    def edges(step, low, high, shift):
        def rows(x, carry):
            write_rows(step, [low + x, high + x], shift)
            return carry

        lax.fori_loop(0, EDGE, rows, 0)

    def products(x, sums):
        sums = list(sums)
        for c in range(6):
            for t in range(2):
                cells = pl.ds(8 * t, 8)
                first = u[c, pl.ds(pl.multiple_of(x * PADY + 8 * t, 8), 8), :]
                values = [first] + [state[c, x, cells, :] for state in states[1:]]
                for number, (i, j) in enumerate(PAIRS):
                    sums[number] = sums[number] + values[i] * values[j]
        return tuple(sums)

    zero = jnp.zeros((8, 128), jnp.float32)

    for copy in copies[:2]:
        copy.wait_recv()
    for number, (f, layer) in enumerate(TO_PREVIOUS):
        u[f, pl.ds(EDGE * PADY + HIGH + layer, OWN, stride=PADY), :] = previous_in[number]
    for number, (f, layer) in enumerate(TO_NEXT):
        u[f, pl.ds(EDGE * PADY + LOW + layer, OWN, stride=PADY), :] = next_in[number]
    interior(1, EDGE + 1, EDGE + OWN, 1)
    interior(2, EDGE + 1, EDGE + OWN - 1, 0)
    interior(3, EDGE + 2, EDGE + OWN - 1, 1)
    interior(4, EDGE + 2, EDGE + OWN - 2, 0)
    sums = lax.fori_loop(EDGE + 2, EDGE + OWN - 2, products, (zero,) * len(PAIRS))

    for copy in copies[2:]:
        copy.wait_recv()
    for f in range(FIELDS):
        for side, first in ((0, EDGE + OWN), (1, 0)):
            for layer in range(2):
                source = face_in[side, f, pl.ds(layer * OWN, OWN), :]
                u[f, pl.ds((first + layer) * PADY, OWN), :] = source
    for number, (side_x, side_y) in enumerate(corners):
        for f in range(FIELDS):
            for layer in range(2):
                x = (EDGE + OWN if side_x == 0 else 0) + layer
                y = HIGH if side_y == 0 else LOW
                if side_x != side_y:
                    source = corner_in[number, pl.ds(f * 4 + layer * 2, 2), :]
                    u[f, pl.ds(x * PADY + y, 2), :] = source
                elif layer == side_x:
                    u[f, pl.ds(x * PADY + y + layer, 1), :] = corner_in[number, pl.ds(f, 1), :]
    edges(1, 1, EDGE + OWN, 1)
    edges(2, 1, EDGE + OWN - 1, 0)
    edges(3, EDGE, EDGE + OWN - 1, 1)
    edges(4, EDGE, EDGE + OWN - 2, 0)
    sums = lax.fori_loop(0, EDGE, lambda i, sums: products(EDGE + i, sums), sums)
    sums = lax.fori_loop(0, EDGE, lambda i, sums: products(OWN + i, sums), sums)
    for number, part in enumerate(sums):
        acc_rows[pl.ds(8 * number, 8), :] = part
    acc_rows[pl.ds(8 * len(PAIRS), 8), :] = zero
    total = acc_rows[pl.ds(0, 16, stride=8), :]
    for s in range(1, 8):
        total = total + acc_rows[pl.ds(s, 16, stride=8), :]
    diagonal = lax.broadcasted_iota(jnp.int32, (16, 128), 0) == lax.broadcasted_iota(jnp.int32, (16, 128), 1)

    def to_row(column):
        return jnp.sum(jnp.where(diagonal, column, 0.0), axis=0, keepdims=True)

    def gather_metal():
        flags = [metal[tile_rows[1 + t // 2], tile_cols[1 + t % 2]] for t in range(4)]
        present = [flag.astype(jnp.float32) for flag in flags]
        before = jnp.float32(0.0)
        chosen = [[None] * 4 for _ in range(MS)]
        for t in range(4):
            taken = [present[t] * (1.0 - before), present[t] * before]
            before = before + present[t]
            for slot in range(MS):
                chosen[slot][t] = taken[slot]

        def rows(x, carry):
            for c in range(3):
                for j, state in enumerate(states[:STEPS]):
                    parts = []
                    for t in range(4):
                        at = EDGE + 8 * (t // 2) + x
                        y = 8 * (t % 2)
                        if j == 0:
                            start_row = pl.multiple_of(at * PADY + y, 8)
                            parts.append(u[c, pl.ds(start_row, 8), :])
                        else:
                            parts.append(state[c, at, pl.ds(y, 8), :])
                    for slot in range(MS):
                        value = chosen[slot][0] * parts[0]
                        for t in range(1, 4):
                            value = value + chosen[slot][t] * parts[t]
                        tiles_out[slot, j, c, x] = value
            return carry

        lax.fori_loop(0, 8, rows, 0)
        for p in range(POLES):
            kicks = [strength[p]]
            kicks.append(-gamma[p] * kicks[0])
            for k in range(2, STEPS):
                kicks.append(-(omega[p] * omega[p]) * kicks[k - 2] - gamma[p] * kicks[k - 1])
            for k in range(STEPS):
                kicks_out[pl.ds(p * STEPS + k, 1), :] = jnp.full((1, 128), kicks[k])

    row = to_row(jnp.sum(total, axis=1, keepdims=True))
    if far:
        pl.semaphore_wait(heard.at[1], len(far))
    me_a = my_core * z_size + my_z
    me_b = my_x * y_size + my_y
    targets_a = [
        device(my_x, ring_core[c], my_y, ring_z[z]) for c, z in farthest_first(cores, z_size)
    ]
    targets_b = [
        device(ring_x[x], my_core, ring_y[y], my_z) for x, y in farthest_first(x_size, y_size)
    ]
    for stage, (slots, me, targets) in enumerate(((sum_a, me_a, targets_a), (sum_b, me_b, targets_b))):
        slots[me] = row
        for target in targets:
            pltpu.make_async_remote_copy(
                src_ref=slots.at[me],
                dst_ref=slots.at[me],
                send_sem=stage_send.at[stage],
                recv_sem=stage_recv.at[stage],
                device_id=target,
                device_id_type=MESH,
            ).start()
        if stage == 0:
            gather_metal()
        settle(slots.at[pl.ds(0, len(targets))], stage_recv.at[stage])
        row = slots[0]
        for member in range(1, len(targets) + 1):
            row = row + slots[member]
    gram_out[...] = jnp.broadcast_to(
        jnp.sum(jnp.where(diagonal, row, 0.0), axis=1, keepdims=True), (16, 128)
    )

    for copy in copies:
        copy.wait_send()
    for stage, (slots, targets) in enumerate(((sum_a, targets_a), (sum_b, targets_b))):
        settle(slots.at[pl.ds(0, len(targets))], stage_send.at[stage])


def finish_kernel(
    cell_count,
    k0,
    k1,
    k2,
    k3,
    k4,
    gram,
    tiles,
    kicks,
    out_e,
    out_h,
    out_poles,
    out_coefficients,
    coefficients,
    table,
    fields,
    poles,
    store_sem,
):
    stores = []

    def store(src, dst):
        copy = pltpu.make_async_copy(src, dst, store_sem.at[len(stores)])
        copy.start()
        stores.append(copy)

    inner = {}
    for number, (i, j) in enumerate(PAIRS):
        inner[i, j] = inner[j, i] = gram[pl.ds(number, 1), :] * (1.0 / cell_count)
    unit = 1.0 / jnp.sqrt(inner[0, 0] + EPSILON)
    weights = [unit]
    lane = lax.broadcasted_iota(jnp.int32, (1, 128), 1)
    for step in range(1, STEPS + 1):
        image = [None] + weights

        def total(terms):
            return functools.reduce(jnp.add, terms)

        along_q = unit * total([image[j] * inner[0, j] for j in range(1, step + 1)])
        rest = [-along_q * unit] + image[1:]
        along_v = jnp.zeros_like(unit)
        if step > 1:
            along_v = total(
                [
                    image[j] * total([weights[i] * inner[i, j] for i in range(step)])
                    for j in range(1, step + 1)
                ]
            )
            for i in range(step):
                rest[i] = rest[i] - along_v * weights[i]
        squared = total(
            [rest[i] * total([rest[j] * inner[i, j] for j in range(step + 1)]) for i in range(step + 1)]
        )
        norm = jnp.sqrt(jnp.maximum(squared, 0.0) + EPSILON)
        scale = 1.0 / norm
        weights = [part * scale for part in rest]
        line = jnp.where(lane == 0, along_q, jnp.where(lane == 1, along_v, norm))
        coefficients[pl.ds(step - 1, 1), :] = line[:, :3]

    store(coefficients, out_coefficients)

    for p in range(POLES):
        kick = [kicks[pl.ds(p * STEPS + k, 1), :] for k in range(STEPS)]
        for j in range(STEPS):
            parts = [weights[k] * kick[k - 1 - j] for k in range(j + 1, STEPS + 1)]
            table[pl.ds(p * 8 + j, 1), :] = functools.reduce(jnp.add, parts)
        for j in range(STEPS - 1):
            parts = [weights[k] * kick[k - 2 - j] for k in range(j + 2, STEPS + 1)]
            table[pl.ds(p * 8 + 4 + j, 1), :] = functools.reduce(jnp.add, parts)
    for j in range(STEPS + 1):
        table[pl.ds(48 + j, 1), :] = weights[j]

    def entry(number):
        return jnp.broadcast_to(table[pl.ds(number, 1), :], (8, 128))

    for slot in range(MS):
        for c in range(3):

            def pole_cells(x, carry):
                field = [tiles[slot, j, c, x] for j in range(STEPS)]
                for p in range(POLES):
                    poles[slot, 1, p, c, x] = functools.reduce(
                        jnp.add, [entry(p * 8 + j) * field[j] for j in range(STEPS)]
                    )
                    poles[slot, 0, p, c, x] = functools.reduce(
                        jnp.add, [entry(p * 8 + 4 + j) * field[j] for j in range(STEPS - 1)]
                    )
                return carry

            lax.fori_loop(0, 8, pole_cells, 0)
            part = (slot, pl.ds(0, 2), pl.ds(0, POLES), c)
            store(poles.at[part], out_poles.at[part])

    for half, out in enumerate((out_e, out_h)):

        def field_cells(x, carry):
            for c in range(3 * half, 3 * half + 3):
                own = pl.ds(pl.multiple_of(x * OWN, 8), OWN)
                value = table[pl.ds(48, 1), :] * k0[c, own, :]
                for j, state in enumerate((k1, k2, k3, k4)):
                    value = value + table[pl.ds(49 + j, 1), :] * state[c, EDGE + x, pl.ds(0, OWN), :]
                fields[c, x] = value
            return carry

        lax.fori_loop(0, OWN, field_cells, 0)
        store(fields.at[pl.ds(3 * half, 3)], out)
    for copy in stores:
        copy.wait()


def body(sizes, u_electric, u_magnetic, eps_inv, metal_map, pole_omega, pole_gamma, pole_strength):
    depth = u_electric.shape[3]
    cell_count = 6.0 * OWN * OWN * depth * sizes[0] * sizes[1] * sizes[2] * sizes[3]
    f32 = jnp.float32
    any_spec = pl.BlockSpec(memory_space=pl.ANY)
    hbm = pl.BlockSpec(memory_space=pltpu.HBM)
    vmem = pl.BlockSpec(memory_space=pltpu.VMEM)
    state = jax.ShapeDtypeStruct((6, PADX, PADY, depth), f32)
    a_size = sizes[1] * sizes[3]
    b_size = sizes[0] * sizes[2]

    def stay(value):
        return pltpu.with_memory_space_constraint(value, pltpu.HBM)

    start = [u_electric.reshape(3, OWN * OWN, depth), u_magnetic.reshape(3, OWN * OWN, depth)]
    model = [stay(part) for part in (metal_map, pole_omega, pole_gamma, pole_strength)]
    dma = pltpu.SemaphoreType.DMA
    results = pl.pallas_call(
        functools.partial(exchange_kernel, sizes, metal_map.shape),
        out_shape=[state] * 4
        + [
            jax.ShapeDtypeStruct((16, depth), f32),
            jax.ShapeDtypeStruct((MS, STEPS, 3, 8, 8, depth), f32),
            jax.ShapeDtypeStruct((POLES * STEPS, depth), f32),
            jax.ShapeDtypeStruct((FIELDS, OWN * OWN, depth), f32),
        ],
        in_specs=[hbm] * 7,
        out_specs=[vmem] * 8,
        scratch_shapes=[
            pltpu.VMEM((2, FIELDS, EDGE * OWN, depth), f32),
            pltpu.VMEM((FIELDS, ROW, depth), f32),
            pltpu.VMEM((len(TO_PREVIOUS), OWN, depth), f32),
            pltpu.VMEM((len(TO_PREVIOUS), OWN, depth), f32),
            pltpu.VMEM((len(TO_NEXT), OWN, depth), f32),
            pltpu.VMEM((len(TO_NEXT), OWN, depth), f32),
            pltpu.VMEM((4, CORNER_ROWS, depth), f32),
            pltpu.VMEM((4, CORNER_ROWS, depth), f32),
            pltpu.VMEM((4, PADY, depth), f32),
            pltpu.VMEM((128, depth), f32),
            pltpu.VMEM((a_size, 1, depth), f32),
            pltpu.VMEM((b_size, 1, depth), f32),
            pltpu.SMEM(metal_map.shape, jnp.int32),
            pltpu.SMEM((POLES,), f32),
            pltpu.SMEM((POLES,), f32),
            pltpu.SMEM((POLES,), f32),
            pltpu.SemaphoreType.REGULAR((2,)),
            dma((7,)),
            dma((8,)),
            dma((8,)),
            dma((2,)),
            dma((2,)),
        ],
        compiler_params=pltpu.CompilerParams(
            collective_id=0, has_side_effects=True, vmem_limit_bytes=VMEM_LIMIT
        ),
    )(*[stay(part) for part in start], stay(eps_inv.reshape(OWN * OWN, depth)), *model)

    k1, k2, k3, k4, gram, tiles, kicks, raw = results

    return pl.pallas_call(
        functools.partial(finish_kernel, cell_count),
        out_shape=[
            jax.ShapeDtypeStruct(u_electric.shape, f32),
            jax.ShapeDtypeStruct(u_magnetic.shape, f32),
            jax.ShapeDtypeStruct((MS, 2, POLES, 3, 8, 8, depth), f32),
            jax.ShapeDtypeStruct((STEPS, 3), f32),
        ],
        in_specs=[vmem] * 8,
        out_specs=[any_spec] * 4,
        scratch_shapes=[
            pltpu.VMEM((STEPS, 3), f32),
            pltpu.VMEM((56, depth), f32),
            pltpu.VMEM((6, OWN, OWN, depth), f32),
            pltpu.VMEM((MS, 2, POLES, 3, 8, 8, depth), f32),
            dma((9,)),
        ],
        compiler_params=pltpu.CompilerParams(vmem_limit_bytes=VMEM_LIMIT),
    )(raw, k1, k2, k3, k4, gram, tiles, kicks)


def solution(mesh):
    sizes = layout(mesh.shape["gx"], mesh.shape["gy"])
    placed = (
        P(None, "gx", "gy", None),
        P(None, "gx", "gy", None),
        P("gx", "gy", None),
        P(),
        P(),
        P(),
        P(),
    )
    return jax.shard_map(
        functools.partial(body, sizes),
        mesh=mesh,
        in_specs=placed,
        out_specs=(
            P(None, "gx", "gy", None),
            P(None, "gx", "gy", None),
            P(("gx", "gy"), None, None, None, None, None, None),
            P(),
        ),
        check_vma=False,
    )
```

time: 875 us -> 32.6 us (0.04)
  blocking collectives: 681 us -> 0 us
  other arithmetic: 70.9 us -> 0 us
  local copies, waits for them, and re-layouts: 52.3 us -> 0 us
  starting transfers between devices: 35.6 us -> 0 us
  Pallas kernels: 0 us -> 31.8 us
  between operations: 31.9 us -> 0.64 us
    psum x9 -> x0, blocking collectives: 681 us -> none  [the longest x4 309 us: body(): lax.psum((field_dot(q_e, q_h, w_e, w_h), field_dot(v_e, v_h, w_e, w_h)),...]
    ppermute x16 -> x0, starting transfers between devices: 35.6 us -> none  [the longest x8 23.9 us: with_halo(): lax.ppermute(tail, axis, [(i, (i + 1) % count) for i in range(count)])]
    pallas_call x0 -> x2, Pallas kernels: none -> 31.8 us  [the longest x1 29.7 us: body(): pl.pallas_call(functools.partial(exchange_kernel, sizes, metal_map.shape)...]
    reduce_sum x18 -> x0, other arithmetic: 28.9 us -> none  [the longest x17 28.2 us: field_dot(): return jnp.sum(first_e * second_e) + jnp.sum(first_h * second_h)]
    concatenate x32 -> x0, local copies, waits for them, and re-layouts: 22.7 us -> none  [the longest x16 11.4 us: behind_z(): return magnetic[component] - jnp.roll(magnetic[component], 1, 2)]
    div x14 -> x0, other arithmetic: 20.2 us -> none  [the longest x4 12.1 us: body(): v_poles = (w_poles - along_v * v_poles) / norm_value]
    slice x32 -> x0, local copies, waits for them, and re-layouts: 17.5 us -> none  [the longest x4 3.12 us: behind_y(): magnetic[component, :, :-1]]
  transfers between devices with their start and end apart: 16 -> 0, of which waited for: 2 -> 0; matrix products, arithmetic and copies ran while one was open for 4% -> 0% of each run, Pallas kernels for 0% -> 0%
where the time goes in v1:
time: 32.6 us; the launch traced here: 32.5 us
  Pallas kernels  31.8 us (98%)
  between operations  0.64 us (2%)
    pallas_call x1, Pallas kernels, body(): pl.pallas_call(functools.partial(exchange_kernel, sizes, metal_map.shape)...  29.7 us
    pallas_call x1, Pallas kernels, body(): pl.pallas_call(functools.partial(finish_kernel, cell_count), out_shape=[j...  2.12 us

profile of v1, /device:TPU:1, one launch (start us, length us, event | category | flops | bytes accessed | tf_op | source)
XLA Modules:
  0.0 32.5 jit_solution(2797000064368326810)
XLA Ops:
  0.6 29.7 %shard_map.102 = (f32[6,20,24,128]{3,2,1,0:T(8,128)S(1)}, f32[6,20,24,128]{3,2,1,0:T(8,128)S(1)}, f32[6,20,24,128]{3,2,1,0:T(8,128)S(1)}, f32[6,20,24,128]{3,2,1...) custom-call(f32[3,256,128]{2,1,0:T(8,128)} %bitcast.3, ...), custom_call_target="tpu_custom_call" | custom-call | tf_op jit(solution)/shard_map/pallas_call | solution.py:578
  30.4 2.1 %shard_map.103 = (f32[3,16,16,128]{3,2,1,0:T(8,128)}, f32[3,16,16,128]{3,2,1,0:T(8,128)}, f32[2,2,6,3,8,8,128]{6,5,4,3,2,1,0:T(8,128)}, f32[4,3]{1,0:T(4,128)}) custom-call(f32[7,256,128]{2,1,0:T(8,128)S(1)} %get-tuple-element.12.k0, f32[6,20,24,128]{3,2,1,0:T(8,128)S(1)} %get-tuple-element.13.k1, f32[6,20,24,128]{3,2,1,0:T(8,128)S(1)} %get-tuple-element.14.k2, ...), custom_call_target="tpu_custom_call" | custom-call | tf_op jit(solution)/shard_map/pallas_call | solution.py:620

commit v2 on v1

--- a/solution.py
+++ b/solution.py
@@ -17,13 +17,16 @@
 OWN = 16
 PADX = OWN + 2 * EDGE
 PADY = 24
-HIGH = 16
-LOW = 22
+HIGH = 18
+LOW = 20
+STRIP = 16
 FIELDS = 7
 TO_PREVIOUS = [(f, 0) for f in range(FIELDS)] + [(f, 1) for f in (0, 2, 3, 4, 5, 6)]
 TO_NEXT = [(f, 1) for f in range(FIELDS)] + [(f, 0) for f in (0, 1, 2, 3, 5)]
 ROW = PADX * PADY
 CORNER_ROWS = 32
+CHUNK = 5
+STRIP_CHUNK = 8
 PAIRS = [(i, j) for i in range(STEPS + 1) for j in range(i, STEPS + 1)]
 VMEM_LIMIT = 40 * 1024 * 1024
 
@@ -81,15 +84,16 @@
     omega_in,
     gamma_in,
     strength_in,
-    k1,
-    k2,
-    k3,
-    k4,
+    own_out,
     gram_out,
     tiles_out,
     kicks_out,
     raw,
     face_in,
+    k1,
+    k2,
+    k3,
+    k4,
     u,
     previous_out,
     previous_in,
@@ -217,14 +221,15 @@
 
     tile_rows = [lax.rem(2 * gx + s - 1 + tiles[0], tiles[0]) for s in range(4)]
     tile_cols = [lax.rem(2 * gy + t - 1 + tiles[1], tiles[1]) for t in range(4)]
-    upper = lax.broadcasted_iota(jnp.int32, (8, 128), 0) < 4
+    place = lax.broadcasted_iota(jnp.int32, (8, 128), 0)
     for s in range(4):
         flag = [
             jnp.full((8, 128), metal[tile_rows[s], tile_cols[t]].astype(jnp.float32)) for t in range(4)
         ]
-        mask[s, 0:8] = flag[1]
-        mask[s, 8:16] = flag[2]
-        mask[s, 16:24] = jnp.where(upper, flag[3], flag[0])
+        mask[s, 0:8] = jnp.where(place < 6, flag[1], flag[2])
+        mask[s, 8:16] = jnp.where(place < 2, flag[1], flag[2])
+        beyond = jnp.where(place < 4, flag[3], flag[0])
+        mask[s, 16:24] = jnp.where(place < 2, flag[2], jnp.where(place < 6, beyond, flag[1]))
 
     response = [jnp.float32(0.0)] * 3
     for p in range(POLES):
@@ -233,10 +238,18 @@
         g2 = -(omega[p] * omega[p]) * g0 - gamma[p] * g1
         response = [response[0] + g0, response[1] + g1, response[2] + g2]
 
+    def put_row(f, x, low, high):
+        first = pl.multiple_of(x * PADY, 8)
+        low_by_6, low_by_2 = pltpu.roll(low, 6, 0), pltpu.roll(low, 2, 0)
+        high_by_6, high_by_2 = pltpu.roll(high, 6, 0), pltpu.roll(high, 2, 0)
+        u[f, pl.ds(first, 8), :] = jnp.where(place < 6, low_by_6, high_by_6)
+        u[f, pl.ds(first + 8, 8), :] = jnp.where(place < 2, low_by_2, high_by_2)
+        u[f, pl.ds(first + 16, 8), :] = jnp.where(place < 4, high_by_2, low_by_6)
+
     def copy_own(x, carry):
+        first = pl.multiple_of(x * OWN, 8)
         for f in range(FIELDS):
-            source = raw[f, pl.ds(pl.multiple_of(x * OWN, 8), OWN), :]
-            u[f, pl.ds(pl.multiple_of((x + EDGE) * PADY, 8), OWN), :] = source
+            put_row(f, x + EDGE, raw[f, pl.ds(first, 8), :], raw[f, pl.ds(first + 8, 8), :])
         return carry
 
     lax.fori_loop(0, OWN, copy_own, 0)
@@ -298,31 +311,138 @@
                 new[3 + c, x - shift] = of_h[c]
 
     def interior(step, low, high, shift):
-        def rows(x, carry):
-            write_rows(step, [x], shift)
+        rest = high - low - CHUNK
+        chunks = -(-rest // CHUNK) + 1
+
+        def rows(i, carry):
+            first = low + (i * rest) // (chunks - 1)
+            write_rows(step, [first + k for k in range(CHUNK)], shift)
             return carry
 
-        lax.fori_loop(low, high, rows, 0)
+        lax.fori_loop(0, chunks, rows, 0)
 
     def edges(step, low, high, shift):
-        def rows(x, carry):
-            write_rows(step, [low + x, high + x], shift)
+        write_rows(step, [low, low + 1, high, high + 1], shift)
+
+    def state_at(j, c, x, first, count):
+        if j == 0:
+            return u[c, pl.ds(x * PADY + first, count), :]
+        return states[j][c, x, pl.ds(first, count), :]
+
+    def strip(j, c, x):
+        if j == 0:
+            return u[c, pl.ds(pl.multiple_of(x * PADY + STRIP, 8), 8), :]
+        return states[j][c, x, pl.ds(STRIP, 8), :]
+
+    def strip_prev(j, c, x, value):
+        return jnp.where(place == 0, state_at(j, c, x, STRIP - 1, 1), pltpu.roll(value, 1, 0))
+
+    def strip_next(j, c, x, value):
+        return jnp.where(place == 7, state_at(j, c, x, 0, 1), pltpu.roll(value, 7, 0))
+
+    def strip_electric(step, x):
+        old = step - 1
+        hx, hy, hz = (strip(old, c, x) for c in (3, 4, 5))
+        hy_back, hz_back = strip(old, 4, x - 1), strip(old, 5, x - 1)
+        curl = [
+            (hz - strip_prev(old, 5, x, hz)) - (hy - prev_z(hy)),
+            (hx - prev_z(hx)) - (hz - hz_back),
+            (hy - hy_back) - (hx - strip_prev(old, 3, x, hx)),
+        ]
+        if step > 1:
+            metal_here = mask[(x + 6) // 8, pl.ds(STRIP, 8), :]
+            for c in range(3):
+                current = response[step - 2] * strip(0, c, x)
+                for j in range(1, step - 1):
+                    current = current + response[step - 2 - j] * strip(j, c, x)
+                curl[c] = curl[c] - metal_here * current
+        eps = strip(0, 6, x)
+        return [eps * part for part in curl]
+
+    def strip_magnetic(step, x):
+        old = step - 1
+        ex, ey, ez = (strip(old, c, x) for c in (0, 1, 2))
+        ey_next, ez_next = strip(old, 1, x + 1), strip(old, 2, x + 1)
+        return [
+            (next_z(ey) - ey) - (strip_next(old, 2, x, ez) - ez),
+            (ez_next - ez) - (next_z(ex) - ex),
+            (strip_next(old, 0, x, ex) - ex) - (ey_next - ey),
+        ]
+
+    def write_strips(step, starts, shift):
+        new = states[step]
+        parts = [(x, strip_electric(step, x), strip_magnetic(step, x - shift)) for x in starts]
+        for x, of_e, of_h in parts:
+            for c in range(3):
+                new[c, x, pl.ds(STRIP, 8), :] = of_e[c]
+                new[3 + c, x - shift, pl.ds(STRIP, 8), :] = of_h[c]
+
+    def interior_strips(step, low, high, shift):
+        rest = high - low - STRIP_CHUNK
+
+        def rows(i, carry):
+            write_strips(step, [low + i * rest + k for k in range(STRIP_CHUNK)], shift)
             return carry
 
-        lax.fori_loop(0, EDGE, rows, 0)
-
-    def products(x, sums):
+        lax.fori_loop(0, 2, rows, 0)
+
+    def edge_strips(step, low, high, shift):
+        write_strips(step, [low, low + 1, high, high + 1], shift)
+
+    zero = jnp.zeros((8, 128), jnp.float32)
+
+    def products(first, x, sums):
         sums = list(sums)
+        cells = pl.ds(first, 8)
         for c in range(6):
-            for t in range(2):
-                cells = pl.ds(8 * t, 8)
-                first = u[c, pl.ds(pl.multiple_of(x * PADY + 8 * t, 8), 8), :]
-                values = [first] + [state[c, x, cells, :] for state in states[1:]]
-                for number, (i, j) in enumerate(PAIRS):
-                    sums[number] = sums[number] + values[i] * values[j]
+            values = [u[c, pl.ds(pl.multiple_of(x * PADY + first, 8), 8), :]]
+            values += [state[c, x, cells, :] for state in states[1:]]
+            for number, (i, j) in enumerate(PAIRS):
+                sums[number] = sums[number] + values[i] * values[j]
         return tuple(sums)
 
-    zero = jnp.zeros((8, 128), jnp.float32)
+    def interior_products(first, sums):
+        return lax.fori_loop(
+            EDGE + 2, EDGE + OWN - 2, lambda x, sums: products(first, x, sums), sums
+        )
+
+    def edge_products(first, sums):
+        return lax.fori_loop(
+            0,
+            2 * EDGE,
+            lambda i, sums: products(first, EDGE + i + i // 2 * (OWN - 4), sums),
+            sums,
+        )
+
+    def keep(sums, wanted, into):
+        for number, part in enumerate(sums):
+            at = pl.ds(8 * number, 8)
+            part = jnp.where(wanted, part, 0.0)
+            acc_rows[at, :] = part + acc_rows[at, :] if into else part
+
+    none = (zero,) * len(PAIRS)
+    interior(1, EDGE + 1, EDGE + OWN, 1)
+    interior(2, EDGE + 1, EDGE + OWN - 1, 0)
+    interior(3, EDGE + 2, EDGE + OWN - 1, 1)
+    interior(4, EDGE + 2, EDGE + OWN - 2, 0)
+    keep(interior_products(0, none), place < 6, False)
+    keep(interior_products(8, none), place >= 2, True)
+    acc_rows[pl.ds(8 * len(PAIRS), 8), :] = zero
+
+    for copy in copies[2:4]:
+        copy.wait_recv()
+    for f in range(FIELDS):
+        for side, first in ((0, EDGE + OWN), (1, 0)):
+            for layer in range(2):
+                low = face_in[side, f, pl.ds(layer * OWN, 8), :]
+                high = face_in[side, f, pl.ds(layer * OWN + 8, 8), :]
+                put_row(f, first + layer, low, high)
+    edges(1, 1, EDGE + OWN, 1)
+    edges(2, 1, EDGE + OWN - 1, 0)
+    edges(3, EDGE, EDGE + OWN - 1, 1)
+    edges(4, EDGE, EDGE + OWN - 2, 0)
+    keep(edge_products(0, none), place < 6, True)
+    keep(edge_products(8, none), place >= 2, True)
 
     for copy in copies[:2]:
         copy.wait_recv()
@@ -330,19 +450,14 @@
         u[f, pl.ds(EDGE * PADY + HIGH + layer, OWN, stride=PADY), :] = previous_in[number]
     for number, (f, layer) in enumerate(TO_NEXT):
         u[f, pl.ds(EDGE * PADY + LOW + layer, OWN, stride=PADY), :] = next_in[number]
-    interior(1, EDGE + 1, EDGE + OWN, 1)
-    interior(2, EDGE + 1, EDGE + OWN - 1, 0)
-    interior(3, EDGE + 2, EDGE + OWN - 1, 1)
-    interior(4, EDGE + 2, EDGE + OWN - 2, 0)
-    sums = lax.fori_loop(EDGE + 2, EDGE + OWN - 2, products, (zero,) * len(PAIRS))
-
-    for copy in copies[2:]:
+    interior_strips(1, EDGE + 1, EDGE + OWN, 1)
+    interior_strips(2, EDGE + 1, EDGE + OWN - 1, 0)
+    interior_strips(3, EDGE + 2, EDGE + OWN - 1, 1)
+    interior_strips(4, EDGE + 2, EDGE + OWN - 2, 0)
+    sums = interior_products(STRIP, none)
+
+    for copy in copies[4:]:
         copy.wait_recv()
-    for f in range(FIELDS):
-        for side, first in ((0, EDGE + OWN), (1, 0)):
-            for layer in range(2):
-                source = face_in[side, f, pl.ds(layer * OWN, OWN), :]
-                u[f, pl.ds((first + layer) * PADY, OWN), :] = source
     for number, (side_x, side_y) in enumerate(corners):
         for f in range(FIELDS):
             for layer in range(2):
@@ -353,15 +468,12 @@
                     u[f, pl.ds(x * PADY + y, 2), :] = source
                 elif layer == side_x:
                     u[f, pl.ds(x * PADY + y + layer, 1), :] = corner_in[number, pl.ds(f, 1), :]
-    edges(1, 1, EDGE + OWN, 1)
-    edges(2, 1, EDGE + OWN - 1, 0)
-    edges(3, EDGE, EDGE + OWN - 1, 1)
-    edges(4, EDGE, EDGE + OWN - 2, 0)
-    sums = lax.fori_loop(0, EDGE, lambda i, sums: products(EDGE + i, sums), sums)
-    sums = lax.fori_loop(0, EDGE, lambda i, sums: products(OWN + i, sums), sums)
-    for number, part in enumerate(sums):
-        acc_rows[pl.ds(8 * number, 8), :] = part
-    acc_rows[pl.ds(8 * len(PAIRS), 8), :] = zero
+    edge_strips(1, 1, EDGE + OWN, 1)
+    edge_strips(2, 1, EDGE + OWN - 1, 0)
+    edge_strips(3, EDGE, EDGE + OWN - 1, 1)
+    edge_strips(4, EDGE, EDGE + OWN - 2, 0)
+    keep(edge_products(STRIP, sums), jnp.logical_or(place < 2, place >= 6), True)
+
     total = acc_rows[pl.ds(0, 16, stride=8), :]
     for s in range(1, 8):
         total = total + acc_rows[pl.ds(s, 16, stride=8), :]
@@ -383,16 +495,15 @@
 
         def rows(x, carry):
             for c in range(3):
-                for j, state in enumerate(states[:STEPS]):
+                for j in range(STEPS):
                     parts = []
                     for t in range(4):
-                        at = EDGE + 8 * (t // 2) + x
+                        at = 8 * (t // 2) + x
                         y = 8 * (t % 2)
                         if j == 0:
-                            start_row = pl.multiple_of(at * PADY + y, 8)
-                            parts.append(u[c, pl.ds(start_row, 8), :])
+                            parts.append(raw[c, pl.ds(pl.multiple_of(at * OWN + y, 8), 8), :])
                         else:
-                            parts.append(state[c, at, pl.ds(y, 8), :])
+                            parts.append(own_out[j - 1, c, at, pl.ds(y, 8), :])
                     for slot in range(MS):
                         value = chosen[slot][0] * parts[0]
                         for t in range(1, 4):
@@ -408,6 +519,21 @@
                 kicks.append(-(omega[p] * omega[p]) * kicks[k - 2] - gamma[p] * kicks[k - 1])
             for k in range(STEPS):
                 kicks_out[pl.ds(p * STEPS + k, 1), :] = jnp.full((1, 128), kicks[k])
+
+    def order_own():
+        def rows(x, carry):
+            for j, state in enumerate(states[1:]):
+                for c in range(6):
+                    tile = [state[c, x + EDGE, pl.ds(8 * t, 8), :] for t in range(3)]
+                    own_out[j, c, x, pl.ds(0, 8), :] = jnp.where(
+                        place < 2, pltpu.roll(tile[2], 2, 0), pltpu.roll(tile[0], 2, 0)
+                    )
+                    own_out[j, c, x, pl.ds(8, 8), :] = jnp.where(
+                        place < 6, pltpu.roll(tile[1], 6, 0), pltpu.roll(tile[2], 6, 0)
+                    )
+            return carry
+
+        lax.fori_loop(0, OWN, rows, 0)
 
     row = to_row(jnp.sum(total, axis=1, keepdims=True))
     if far:
@@ -432,6 +558,8 @@
                 device_id_type=MESH,
             ).start()
         if stage == 0:
+            order_own()
+        else:
             gather_metal()
         settle(slots.at[pl.ds(0, len(targets))], stage_recv.at[stage])
         row = slots[0]
@@ -450,10 +578,7 @@
 def finish_kernel(
     cell_count,
     k0,
-    k1,
-    k2,
-    k3,
-    k4,
+    own,
     gram,
     tiles,
     kicks,
@@ -465,6 +590,7 @@
     table,
     fields,
     poles,
+    pole_sem,
     store_sem,
 ):
     stores = []
@@ -523,37 +649,43 @@
     def entry(number):
         return jnp.broadcast_to(table[pl.ds(number, 1), :], (8, 128))
 
-    for slot in range(MS):
-        for c in range(3):
-
-            def pole_cells(x, carry):
-                field = [tiles[slot, j, c, x] for j in range(STEPS)]
-                for p in range(POLES):
-                    poles[slot, 1, p, c, x] = functools.reduce(
-                        jnp.add, [entry(p * 8 + j) * field[j] for j in range(STEPS)]
-                    )
-                    poles[slot, 0, p, c, x] = functools.reduce(
-                        jnp.add, [entry(p * 8 + 4 + j) * field[j] for j in range(STEPS - 1)]
-                    )
-                return carry
-
-            lax.fori_loop(0, 8, pole_cells, 0)
-            part = (slot, pl.ds(0, 2), pl.ds(0, POLES), c)
-            store(poles.at[part], out_poles.at[part])
+    def pole_part(i):
+        return (i // 3, pl.ds(0, 2), pl.ds(0, POLES), i % 3)
+
+    def pole_cells(i, carry):
+        slot, c = i // 3, i % 3
+        for x in range(8):
+            field = [tiles[slot, j, c, x] for j in range(STEPS)]
+            for p in range(POLES):
+                poles[slot, 1, p, c, x] = functools.reduce(
+                    jnp.add, [entry(p * 8 + j) * field[j] for j in range(STEPS)]
+                )
+                poles[slot, 0, p, c, x] = functools.reduce(
+                    jnp.add, [entry(p * 8 + 4 + j) * field[j] for j in range(STEPS - 1)]
+                )
+        pltpu.make_async_copy(
+            poles.at[pole_part(i)], out_poles.at[pole_part(i)], pole_sem.at[i]
+        ).start()
+        return carry
+
+    lax.fori_loop(0, 3 * MS, pole_cells, 0)
 
     for half, out in enumerate((out_e, out_h)):
 
-        def field_cells(x, carry):
-            for c in range(3 * half, 3 * half + 3):
-                own = pl.ds(pl.multiple_of(x * OWN, 8), OWN)
-                value = table[pl.ds(48, 1), :] * k0[c, own, :]
-                for j, state in enumerate((k1, k2, k3, k4)):
-                    value = value + table[pl.ds(49 + j, 1), :] * state[c, EDGE + x, pl.ds(0, OWN), :]
-                fields[c, x] = value
+        def field_cells(i, carry):
+            for x in [4 * i + k for k in range(4)]:
+                for c in range(3 * half, 3 * half + 3):
+                    cells = pl.ds(pl.multiple_of(x * OWN, 8), OWN)
+                    value = table[pl.ds(48, 1), :] * k0[c, cells, :]
+                    for j in range(STEPS):
+                        value = value + table[pl.ds(49 + j, 1), :] * own[j, c, x]
+                    fields[c, x] = value
             return carry
 
-        lax.fori_loop(0, OWN, field_cells, 0)
+        lax.fori_loop(0, OWN // 4, field_cells, 0)
         store(fields.at[pl.ds(3 * half, 3)], out)
+    for i in range(3 * MS):
+        pltpu.make_async_copy(poles.at[pole_part(i)], out_poles.at[pole_part(i)], pole_sem.at[i]).wait()
     for copy in stores:
         copy.wait()
 
@@ -565,7 +697,6 @@
     any_spec = pl.BlockSpec(memory_space=pl.ANY)
     hbm = pl.BlockSpec(memory_space=pltpu.HBM)
     vmem = pl.BlockSpec(memory_space=pltpu.VMEM)
-    state = jax.ShapeDtypeStruct((6, PADX, PADY, depth), f32)
     a_size = sizes[1] * sizes[3]
     b_size = sizes[0] * sizes[2]
 
@@ -577,17 +708,18 @@
     dma = pltpu.SemaphoreType.DMA
     results = pl.pallas_call(
         functools.partial(exchange_kernel, sizes, metal_map.shape),
-        out_shape=[state] * 4
-        + [
+        out_shape=[
+            jax.ShapeDtypeStruct((STEPS, 6, OWN, OWN, depth), f32),
             jax.ShapeDtypeStruct((16, depth), f32),
             jax.ShapeDtypeStruct((MS, STEPS, 3, 8, 8, depth), f32),
             jax.ShapeDtypeStruct((POLES * STEPS, depth), f32),
             jax.ShapeDtypeStruct((FIELDS, OWN * OWN, depth), f32),
         ],
         in_specs=[hbm] * 7,
-        out_specs=[vmem] * 8,
+        out_specs=[vmem] * 5,
         scratch_shapes=[
             pltpu.VMEM((2, FIELDS, EDGE * OWN, depth), f32),
+            *[pltpu.VMEM((6, PADX, PADY, depth), f32)] * STEPS,
             pltpu.VMEM((FIELDS, ROW, depth), f32),
             pltpu.VMEM((len(TO_PREVIOUS), OWN, depth), f32),
             pltpu.VMEM((len(TO_PREVIOUS), OWN, depth), f32),
@@ -615,7 +747,7 @@
         ),
     )(*[stay(part) for part in start], stay(eps_inv.reshape(OWN * OWN, depth)), *model)
 
-    k1, k2, k3, k4, gram, tiles, kicks, raw = results
+    own, gram, tiles, kicks, raw = results
 
     return pl.pallas_call(
         functools.partial(finish_kernel, cell_count),
@@ -625,17 +757,18 @@
             jax.ShapeDtypeStruct((MS, 2, POLES, 3, 8, 8, depth), f32),
             jax.ShapeDtypeStruct((STEPS, 3), f32),
         ],
-        in_specs=[vmem] * 8,
+        in_specs=[vmem] * 5,
         out_specs=[any_spec] * 4,
         scratch_shapes=[
             pltpu.VMEM((STEPS, 3), f32),
             pltpu.VMEM((56, depth), f32),
             pltpu.VMEM((6, OWN, OWN, depth), f32),
             pltpu.VMEM((MS, 2, POLES, 3, 8, 8, depth), f32),
-            dma((9,)),
+            dma((3 * MS,)),
+            dma((3,)),
         ],
         compiler_params=pltpu.CompilerParams(vmem_limit_bytes=VMEM_LIMIT),
-    )(raw, k1, k2, k3, k4, gram, tiles, kicks)
+    )(raw, own, gram, tiles, kicks)
 
 
 def solution(mesh):

time: 32.6 us -> 27.9 us (0.86)
  Pallas kernels: 31.8 us -> 27.1 us
    pallas_call x1, Pallas kernels: 29.7 us -> 25.2 us  [body(): pl.pallas_call(functools.partial(exchange_kernel, sizes, metal_map.shape)...]
where the time goes in v2:
time: 27.9 us; the launch traced here: 27.8 us
  Pallas kernels  27.1 us (97%)
  between operations  0.64 us (2%)
    pallas_call x1, Pallas kernels, body(): pl.pallas_call(functools.partial(exchange_kernel, sizes, metal_map.shape)...  25.2 us
    pallas_call x1, Pallas kernels, body(): pl.pallas_call(functools.partial(finish_kernel, cell_count), out_shape=[j...  1.98 us

profile of v2, /device:TPU:1, one launch (start us, length us, event | category | flops | bytes accessed | tf_op | source)
XLA Modules:
  0.0 27.8 jit_solution(18038339121290162215)
XLA Ops:
  0.6 25.2 %shard_map.102 = (f32[4,6,16,16,128]{4,3,2,1,0:T(8,128)S(1)}, f32[16,128]{1,0:T(8,128)S(1)}, f32[2,4,3,8,8,128]{5,4,3,2,1,0:T(8,128)S(1)}, f32[24,128]{1,0:T(8,128)S(1)}, f32[7,256,128]{2,1,0:T(8,128)S(1)}) custom-call(f32[3,256,128]{2,1,0:T(8,128)} %bitcast.3, f32[3,256,128]{2,1,0:T(8,128)} %bitcast.4, f32[256,128]{1,0:T(8,128)} %bitcast.5, ...), custom_call_target="tpu_custom_call" | custom-call | tf_op jit(solution)/shard_map/pallas_call | solution.py:709
  25.8 2.0 %shard_map.103 = (f32[3,16,16,128]{3,2,1,0:T(8,128)}, f32[3,16,16,128]{3,2,1,0:T(8,128)}, f32[2,2,6,3,8,8,128]{6,5,4,3,2,1,0:T(8,128)}, f32[4,3]{1,0:T(4,128)}) custom-call(f32[7,256,128]{2,1,0:T(8,128)S(1)} %get-tuple-element.9.k0, f32[4,6,16,16,128]{4,3,2,1,0:T(8,128)S(1)} %get-tuple-element.10.own, f32[16,128]{1,0:T(8,128)S(1)} %get-tuple-element.11.gram, ...), custom_call_target="tpu_custom_call" | custom-call | tf_op jit(solution)/shard_map/pallas_call | solution.py:752

commit v3 on v2

--- a/solution.py
+++ b/solution.py
@@ -26,7 +26,6 @@
 ROW = PADX * PADY
 CORNER_ROWS = 32
 CHUNK = 5
-STRIP_CHUNK = 8
 PAIRS = [(i, j) for i in range(STEPS + 1) for j in range(i, STEPS + 1)]
 VMEM_LIMIT = 40 * 1024 * 1024
 
@@ -378,13 +377,7 @@
                 new[3 + c, x - shift, pl.ds(STRIP, 8), :] = of_h[c]
 
     def interior_strips(step, low, high, shift):
-        rest = high - low - STRIP_CHUNK
-
-        def rows(i, carry):
-            write_strips(step, [low + i * rest + k for k in range(STRIP_CHUNK)], shift)
-            return carry
-
-        lax.fori_loop(0, 2, rows, 0)
+        write_strips(step, list(range(low, high)), shift)
 
     def edge_strips(step, low, high, shift):
         write_strips(step, [low, low + 1, high, high + 1], shift)
@@ -399,6 +392,20 @@
             values += [state[c, x, cells, :] for state in states[1:]]
             for number, (i, j) in enumerate(PAIRS):
                 sums[number] = sums[number] + values[i] * values[j]
+        return tuple(sums)
+
+    ends = jnp.logical_or(place < 2, place >= 6)
+
+    def strip_products(pairs, sums):
+        sums = list(sums)
+        for x, other in pairs:
+            for c in range(6):
+                values = [
+                    jnp.where(ends, strip(j, c, x), pltpu.roll(strip(j, c, other), 4, 0))
+                    for j in range(STEPS + 1)
+                ]
+                for number, (i, j) in enumerate(PAIRS):
+                    sums[number] = sums[number] + values[i] * values[j]
         return tuple(sums)
 
     def interior_products(first, sums):
@@ -454,7 +461,12 @@
     interior_strips(2, EDGE + 1, EDGE + OWN - 1, 0)
     interior_strips(3, EDGE + 2, EDGE + OWN - 1, 1)
     interior_strips(4, EDGE + 2, EDGE + OWN - 2, 0)
-    sums = interior_products(STRIP, none)
+    sums = lax.fori_loop(
+        0,
+        3,
+        lambda i, sums: strip_products([(4 + 4 * i, 5 + 4 * i), (6 + 4 * i, 7 + 4 * i)], sums),
+        none,
+    )
 
     for copy in copies[4:]:
         copy.wait_recv()
@@ -472,7 +484,7 @@
     edge_strips(2, 1, EDGE + OWN - 1, 0)
     edge_strips(3, EDGE, EDGE + OWN - 1, 1)
     edge_strips(4, EDGE, EDGE + OWN - 2, 0)
-    keep(edge_products(STRIP, sums), jnp.logical_or(place < 2, place >= 6), True)
+    keep(strip_products([(2, 3), (16, 17)], sums), place < 8, True)
 
     total = acc_rows[pl.ds(0, 16, stride=8), :]
     for s in range(1, 8):

time: 27.9 us -> 27.1 us (0.971)
  Pallas kernels: 27.1 us -> 26.4 us
    pallas_call x1, Pallas kernels: 25.2 us -> 24.4 us  [body(): pl.pallas_call(functools.partial(exchange_kernel, sizes, metal_map.shape)...]
where the time goes in v3:
time: 27.1 us; the launch traced here: 27 us
  Pallas kernels  26.4 us (97%)
  between operations  0.64 us (2%)
    pallas_call x1, Pallas kernels, body(): pl.pallas_call(functools.partial(exchange_kernel, sizes, metal_map.shape)...  24.4 us
    pallas_call x1, Pallas kernels, body(): pl.pallas_call(functools.partial(finish_kernel, cell_count), out_shape=[j...  1.98 us

profile of v3, /device:TPU:1, one launch (start us, length us, event | category | flops | bytes accessed | tf_op | source)
XLA Modules:
  0.0 27.0 jit_solution(7492720556644274074)
XLA Ops:
  0.6 24.4 %shard_map.102 = (f32[4,6,16,16,128]{4,3,2,1,0:T(8,128)S(1)}, f32[16,128]{1,0:T(8,128)S(1)}, f32[2,4,3,8,8,128]{5,4,3,2,1,0:T(8,128)S(1)}, f32[24,128]{1,0:T(8,128)S(1)}, f32[7,256,128]{2,1,0:T(8,128)S(1)}) custom-call(f32[3,256,128]{2,1,0:T(8,128)} %bitcast.3, f32[3,256,128]{2,1,0:T(8,128)} %bitcast.4, f32[256,128]{1,0:T(8,128)} %bitcast.5, ...), custom_call_target="tpu_custom_call" | custom-call | tf_op jit(solution)/shard_map/pallas_call | solution.py:721
  25.1 2.0 %shard_map.103 = (f32[3,16,16,128]{3,2,1,0:T(8,128)}, f32[3,16,16,128]{3,2,1,0:T(8,128)}, f32[2,2,6,3,8,8,128]{6,5,4,3,2,1,0:T(8,128)}, f32[4,3]{1,0:T(4,128)}) custom-call(f32[7,256,128]{2,1,0:T(8,128)S(1)} %get-tuple-element.9.k0, f32[4,6,16,16,128]{4,3,2,1,0:T(8,128)S(1)} %get-tuple-element.10.own, f32[16,128]{1,0:T(8,128)S(1)} %get-tuple-element.11.gram, ...), custom_call_target="tpu_custom_call" | custom-call | tf_op jit(solution)/shard_map/pallas_call | solution.py:764

commit v4 on v3

--- a/solution.py
+++ b/solution.py
@@ -461,12 +461,6 @@
     interior_strips(2, EDGE + 1, EDGE + OWN - 1, 0)
     interior_strips(3, EDGE + 2, EDGE + OWN - 1, 1)
     interior_strips(4, EDGE + 2, EDGE + OWN - 2, 0)
-    sums = lax.fori_loop(
-        0,
-        3,
-        lambda i, sums: strip_products([(4 + 4 * i, 5 + 4 * i), (6 + 4 * i, 7 + 4 * i)], sums),
-        none,
-    )
 
     for copy in copies[4:]:
         copy.wait_recv()
@@ -484,6 +478,7 @@
     edge_strips(2, 1, EDGE + OWN - 1, 0)
     edge_strips(3, EDGE, EDGE + OWN - 1, 1)
     edge_strips(4, EDGE, EDGE + OWN - 2, 0)
+    sums = strip_products([(x, x + 1) for x in range(EDGE + 2, EDGE + OWN - 2, 2)], none)
     keep(strip_products([(2, 3), (16, 17)], sums), place < 8, True)
 
     total = acc_rows[pl.ds(0, 16, stride=8), :]
@@ -666,14 +661,16 @@
 
     def pole_cells(i, carry):
         slot, c = i // 3, i % 3
-        for x in range(8):
-            field = [tiles[slot, j, c, x] for j in range(STEPS)]
-            for p in range(POLES):
+        field = [[tiles[slot, j, c, x] for j in range(STEPS)] for x in range(8)]
+        for p in range(POLES):
+            for_j = [entry(p * 8 + j) for j in range(STEPS)]
+            for_p = [entry(p * 8 + 4 + j) for j in range(STEPS - 1)]
+            for x in range(8):
                 poles[slot, 1, p, c, x] = functools.reduce(
-                    jnp.add, [entry(p * 8 + j) * field[j] for j in range(STEPS)]
+                    jnp.add, [weight * part for weight, part in zip(for_j, field[x])]
                 )
                 poles[slot, 0, p, c, x] = functools.reduce(
-                    jnp.add, [entry(p * 8 + 4 + j) * field[j] for j in range(STEPS - 1)]
+                    jnp.add, [weight * part for weight, part in zip(for_p, field[x])]
                 )
         pltpu.make_async_copy(
             poles.at[pole_part(i)], out_poles.at[pole_part(i)], pole_sem.at[i]

time: 27.1 us -> 27 us (level)
  no operation moved by 1% of the time
where the time goes in v4:
time: 27 us; the launch traced here: 26.9 us
  Pallas kernels  26.3 us (97%)
  between operations  0.64 us (2%)
    pallas_call x1, Pallas kernels, body(): pl.pallas_call(functools.partial(exchange_kernel, sizes, metal_map.shape)...  24.3 us
    pallas_call x1, Pallas kernels, body(): pl.pallas_call(functools.partial(finish_kernel, cell_count), out_shape=[j...  1.98 us

profile of v4, /device:TPU:1, one launch (start us, length us, event | category | flops | bytes accessed | tf_op | source)
XLA Modules:
  0.0 26.9 jit_solution(7820726357451983836)
XLA Ops:
  0.6 24.3 %shard_map.102 = (f32[4,6,16,16,128]{4,3,2,1,0:T(8,128)S(1)}, f32[16,128]{1,0:T(8,128)S(1)}, f32[2,4,3,8,8,128]{5,4,3,2,1,0:T(8,128)S(1)}, f32[24,128]{1,0:T(8,128)S(1)}, f32[7,256,128]{2,1,0:T(8,128)S(1)}) custom-call(f32[3,256,128]{2,1,0:T(8,128)} %bitcast.3, f32[3,256,128]{2,1,0:T(8,128)} %bitcast.4, f32[256,128]{1,0:T(8,128)} %bitcast.5, ...), custom_call_target="tpu_custom_call" | custom-call | tf_op jit(solution)/shard_map/pallas_call | solution.py:718
  24.9 2.0 %shard_map.103 = (f32[3,16,16,128]{3,2,1,0:T(8,128)}, f32[3,16,16,128]{3,2,1,0:T(8,128)}, f32[2,2,6,3,8,8,128]{6,5,4,3,2,1,0:T(8,128)}, f32[4,3]{1,0:T(4,128)}) custom-call(f32[7,256,128]{2,1,0:T(8,128)S(1)} %get-tuple-element.9.k0, f32[4,6,16,16,128]{4,3,2,1,0:T(8,128)S(1)} %get-tuple-element.10.own, f32[16,128]{1,0:T(8,128)S(1)} %get-tuple-element.11.gram, ...), custom_call_target="tpu_custom_call" | custom-call | tf_op jit(solution)/shard_map/pallas_call | solution.py:761

commit v5 on v3

--- a/solution.py
+++ b/solution.py
@@ -129,9 +129,6 @@
         pltpu.make_async_copy(gamma_in, gamma, load_sem.at[5]),
         pltpu.make_async_copy(strength_in, strength, load_sem.at[6]),
     ]
-    for load in loads:
-        load.start()
-
     def ring(position, size):
         return [position] + [lax.rem(position + step, size) for step in range(1, size)]
 
@@ -169,6 +166,8 @@
         signal(barrier, neighbour(dx, dy))
     for place in near:
         signal(barrier, along(*place))
+    for load in loads:
+        load.start()
 
     for load in loads:
         load.wait()
@@ -379,9 +378,6 @@
     def interior_strips(step, low, high, shift):
         write_strips(step, list(range(low, high)), shift)
 
-    def edge_strips(step, low, high, shift):
-        write_strips(step, [low, low + 1, high, high + 1], shift)
-
     zero = jnp.zeros((8, 128), jnp.float32)
 
     def products(first, x, sums):
@@ -435,21 +431,6 @@
     keep(interior_products(0, none), place < 6, False)
     keep(interior_products(8, none), place >= 2, True)
     acc_rows[pl.ds(8 * len(PAIRS), 8), :] = zero
-
-    for copy in copies[2:4]:
-        copy.wait_recv()
-    for f in range(FIELDS):
-        for side, first in ((0, EDGE + OWN), (1, 0)):
-            for layer in range(2):
-                low = face_in[side, f, pl.ds(layer * OWN, 8), :]
-                high = face_in[side, f, pl.ds(layer * OWN + 8, 8), :]
-                put_row(f, first + layer, low, high)
-    edges(1, 1, EDGE + OWN, 1)
-    edges(2, 1, EDGE + OWN - 1, 0)
-    edges(3, EDGE, EDGE + OWN - 1, 1)
-    edges(4, EDGE, EDGE + OWN - 2, 0)
-    keep(edge_products(0, none), place < 6, True)
-    keep(edge_products(8, none), place >= 2, True)
 
     for copy in copies[:2]:
         copy.wait_recv()
@@ -468,8 +449,14 @@
         none,
     )
 
-    for copy in copies[4:]:
+    for copy in copies[2:]:
         copy.wait_recv()
+    for f in range(FIELDS):
+        for side, first in ((0, EDGE + OWN), (1, 0)):
+            for layer in range(2):
+                low = face_in[side, f, pl.ds(layer * OWN, 8), :]
+                high = face_in[side, f, pl.ds(layer * OWN + 8, 8), :]
+                put_row(f, first + layer, low, high)
     for number, (side_x, side_y) in enumerate(corners):
         for f in range(FIELDS):
             for layer in range(2):
@@ -480,10 +467,12 @@
                     u[f, pl.ds(x * PADY + y, 2), :] = source
                 elif layer == side_x:
                     u[f, pl.ds(x * PADY + y + layer, 1), :] = corner_in[number, pl.ds(f, 1), :]
-    edge_strips(1, 1, EDGE + OWN, 1)
-    edge_strips(2, 1, EDGE + OWN - 1, 0)
-    edge_strips(3, EDGE, EDGE + OWN - 1, 1)
-    edge_strips(4, EDGE, EDGE + OWN - 2, 0)
+    edges(1, 1, EDGE + OWN, 1)
+    edges(2, 1, EDGE + OWN - 1, 0)
+    edges(3, EDGE, EDGE + OWN - 1, 1)
+    edges(4, EDGE, EDGE + OWN - 2, 0)
+    keep(edge_products(0, none), place < 6, True)
+    keep(edge_products(8, none), place >= 2, True)
     keep(strip_products([(2, 3), (16, 17)], sums), place < 8, True)
 
     total = acc_rows[pl.ds(0, 16, stride=8), :]

time: 27.1 us -> 27.6 us (1.018)
  Pallas kernels: 26.4 us -> 26.9 us
    pallas_call x1, Pallas kernels: 24.4 us -> 24.9 us  [body(): pl.pallas_call(functools.partial(exchange_kernel, sizes, metal_map.shape)...]
where the time goes in v5:
time: 27.6 us; the launch traced here: 27.5 us
  Pallas kernels  26.9 us (97%)
  between operations  0.64 us (2%)
    pallas_call x1, Pallas kernels, body(): pl.pallas_call(functools.partial(exchange_kernel, sizes, metal_map.shape)...  24.9 us
    pallas_call x1, Pallas kernels, body(): pl.pallas_call(functools.partial(finish_kernel, cell_count), out_shape=[j...  1.98 us

profile of v5, /device:TPU:1, one launch (start us, length us, event | category | flops | bytes accessed | tf_op | source)
XLA Modules:
  0.0 27.5 jit_solution(6525698969483151989)
XLA Ops:
  0.6 24.9 %shard_map.102 = (f32[4,6,16,16,128]{4,3,2,1,0:T(8,128)S(1)}, f32[16,128]{1,0:T(8,128)S(1)}, f32[2,4,3,8,8,128]{5,4,3,2,1,0:T(8,128)S(1)}, f32[24,128]{1,0:T(8,128)S(1)}, f32[7,256,128]{2,1,0:T(8,128)S(1)}) custom-call(f32[3,256,128]{2,1,0:T(8,128)} %bitcast.3, f32[3,256,128]{2,1,0:T(8,128)} %bitcast.4, f32[256,128]{1,0:T(8,128)} %bitcast.5, ...), custom_call_target="tpu_custom_call" | custom-call | tf_op jit(solution)/shard_map/pallas_call | solution.py:710
  25.5 2.0 %shard_map.103 = (f32[3,16,16,128]{3,2,1,0:T(8,128)}, f32[3,16,16,128]{3,2,1,0:T(8,128)}, f32[2,2,6,3,8,8,128]{6,5,4,3,2,1,0:T(8,128)}, f32[4,3]{1,0:T(4,128)}) custom-call(f32[7,256,128]{2,1,0:T(8,128)S(1)} %get-tuple-element.9.k0, f32[4,6,16,16,128]{4,3,2,1,0:T(8,128)S(1)} %get-tuple-element.10.own, f32[16,128]{1,0:T(8,128)S(1)} %get-tuple-element.11.gram, ...), custom_call_target="tpu_custom_call" | custom-call | tf_op jit(solution)/shard_map/pallas_call | solution.py:753

commit v6 on v5

--- a/solution.py
+++ b/solution.py
@@ -157,7 +157,9 @@
     def signal(semaphore, target):
         pl.semaphore_signal(semaphore, inc=1, device_id=target, device_id_type=MESH)
 
-    beside = [(0, -1), (0, 1), (-1, 0), (1, 0)]
+    corners = [(0, 0), (0, 1), (1, 0), (1, 1)]
+    beside = [(2 * side_x - 1, 2 * side_y - 1) for side_x, side_y in corners]
+    beside += [(0, -1), (0, 1), (-1, 0), (1, 0)]
     near = [(axis, step, 0) for axis, _, steps, _ in rings(sizes) for step in steps]
     near += [(axis, step, 1) for axis, step, _ in near if axis == "z"]
     far = [(axis, step) for axis, _, _, steps in rings(sizes) for step in steps]
@@ -176,7 +178,6 @@
         previous_out[number] = raw[f, pl.ds(layer, OWN, stride=OWN), :]
     for number, (f, layer) in enumerate(TO_NEXT):
         next_out[number] = raw[f, pl.ds(OWN - 2 + layer, OWN, stride=OWN), :]
-    corners = [(0, 0), (0, 1), (1, 0), (1, 1)]
     for number, (side_x, side_y) in enumerate(corners):
         for f in range(FIELDS):
             for layer in range(2):
@@ -208,12 +209,17 @@
 
     send(previous_out, previous_in, neighbour(0, -1))
     send(next_out, next_in, neighbour(0, 1))
+    for number, (side_x, side_y) in enumerate(corners):
+        rows = pl.ds(0, 8 if side_x == side_y else CORNER_ROWS)
+        send(
+            corner_out.at[number, rows],
+            corner_in.at[number, rows],
+            neighbour(2 * side_x - 1, 2 * side_y - 1),
+        )
     everything = pl.ds(0, FIELDS)
     layers = EDGE * OWN
     send(raw.at[everything, pl.ds(0, layers)], face_in.at[0], neighbour(-1, 0))
     send(raw.at[everything, pl.ds(OWN * OWN - layers, layers)], face_in.at[1], neighbour(1, 0))
-    for dx, dy in beside[2:]:
-        signal(heard.at[0], neighbour(dx, dy))
     for place in near:
         signal(heard.at[0], along(*place))
 
@@ -252,17 +258,9 @@
 
     lax.fori_loop(0, OWN, copy_own, 0)
 
-    pl.semaphore_wait(heard.at[0], len(beside[2:]) + len(near))
+    pl.semaphore_wait(heard.at[0], len(near))
     for axis, step in far:
         signal(heard.at[1], along(axis, step))
-    for number, (side_x, side_y) in enumerate(corners):
-        rows = pl.ds(0, 8 if side_x == side_y else CORNER_ROWS)
-        send(
-            corner_out.at[number, rows],
-            corner_in.at[number, rows],
-            neighbour(2 * side_x - 1, 2 * side_y - 1),
-        )
-
     class Padded:
         def __getitem__(self, at):
             f, x = at

time: 27.6 us -> 28.4 us (1.029)
  Pallas kernels: 26.9 us -> 27.7 us
    pallas_call x1, Pallas kernels: 24.9 us -> 25.7 us  [body(): pl.pallas_call(functools.partial(exchange_kernel, sizes, metal_map.shape)...]
where the time goes in v6:
time: 28.4 us; the launch traced here: 28.3 us
  Pallas kernels  27.7 us (98%)
  between operations  0.64 us (2%)
    pallas_call x1, Pallas kernels, body(): pl.pallas_call(functools.partial(exchange_kernel, sizes, metal_map.shape)...  25.7 us
    pallas_call x1, Pallas kernels, body(): pl.pallas_call(functools.partial(finish_kernel, cell_count), out_shape=[j...  1.98 us

profile of v6, /device:TPU:1, one launch (start us, length us, event | category | flops | bytes accessed | tf_op | source)
XLA Modules:
  0.0 28.3 jit_solution(18106748572883080258)
XLA Ops:
  0.6 25.7 %shard_map.102 = (f32[4,6,16,16,128]{4,3,2,1,0:T(8,128)S(1)}, f32[16,128]{1,0:T(8,128)S(1)}, f32[2,4,3,8,8,128]{5,4,3,2,1,0:T(8,128)S(1)}, f32[24,128]{1,0:T(8,128)S(1)}, f32[7,256,128]{2,1,0:T(8,128)S(1)}) custom-call(f32[3,256,128]{2,1,0:T(8,128)} %bitcast.3, f32[3,256,128]{2,1,0:T(8,128)} %bitcast.4, f32[256,128]{1,0:T(8,128)} %bitcast.5, ...), custom_call_target="tpu_custom_call" | custom-call | tf_op jit(solution)/shard_map/pallas_call | solution.py:708
  26.3 2.0 %shard_map.103 = (f32[3,16,16,128]{3,2,1,0:T(8,128)}, f32[3,16,16,128]{3,2,1,0:T(8,128)}, f32[2,2,6,3,8,8,128]{6,5,4,3,2,1,0:T(8,128)}, f32[4,3]{1,0:T(4,128)}) custom-call(f32[7,256,128]{2,1,0:T(8,128)S(1)} %get-tuple-element.9.k0, f32[4,6,16,16,128]{4,3,2,1,0:T(8,128)S(1)} %get-tuple-element.10.own, f32[16,128]{1,0:T(8,128)S(1)} %get-tuple-element.11.gram, ...), custom_call_target="tpu_custom_call" | custom-call | tf_op jit(solution)/shard_map/pallas_call | solution.py:751

commit v7 on v3

--- a/solution.py
+++ b/solution.py
@@ -214,7 +214,7 @@
     send(raw.at[everything, pl.ds(0, layers)], face_in.at[0], neighbour(-1, 0))
     send(raw.at[everything, pl.ds(OWN * OWN - layers, layers)], face_in.at[1], neighbour(1, 0))
     for dx, dy in beside[2:]:
-        signal(heard.at[0], neighbour(dx, dy))
+        signal(heard.at[2], neighbour(dx, dy))
     for place in near:
         signal(heard.at[0], along(*place))
 
@@ -252,17 +252,6 @@
         return carry
 
     lax.fori_loop(0, OWN, copy_own, 0)
-
-    pl.semaphore_wait(heard.at[0], len(beside[2:]) + len(near))
-    for axis, step in far:
-        signal(heard.at[1], along(axis, step))
-    for number, (side_x, side_y) in enumerate(corners):
-        rows = pl.ds(0, 8 if side_x == side_y else CORNER_ROWS)
-        send(
-            corner_out.at[number, rows],
-            corner_in.at[number, rows],
-            neighbour(2 * side_x - 1, 2 * side_y - 1),
-        )
 
     class Padded:
         def __getitem__(self, at):
@@ -432,6 +421,17 @@
     interior(2, EDGE + 1, EDGE + OWN - 1, 0)
     interior(3, EDGE + 2, EDGE + OWN - 1, 1)
     interior(4, EDGE + 2, EDGE + OWN - 2, 0)
+    pl.semaphore_wait(heard.at[2], len(beside[2:]))
+    for number, (side_x, side_y) in enumerate(corners):
+        rows = pl.ds(0, 8 if side_x == side_y else CORNER_ROWS)
+        send(
+            corner_out.at[number, rows],
+            corner_in.at[number, rows],
+            neighbour(2 * side_x - 1, 2 * side_y - 1),
+        )
+    pl.semaphore_wait(heard.at[0], len(near))
+    for axis, step in far:
+        signal(heard.at[1], along(axis, step))
     keep(interior_products(0, none), place < 6, False)
     keep(interior_products(8, none), place >= 2, True)
     acc_rows[pl.ds(8 * len(PAIRS), 8), :] = zero
@@ -747,7 +747,7 @@
             pltpu.SMEM((POLES,), f32),
             pltpu.SMEM((POLES,), f32),
             pltpu.SMEM((POLES,), f32),
-            pltpu.SemaphoreType.REGULAR((2,)),
+            pltpu.SemaphoreType.REGULAR((3,)),
             dma((7,)),
             dma((8,)),
             dma((8,)),

time: 27.1 us -> 27.1 us (level)
  no operation moved by 1% of the time
where the time goes in v7:
time: 27.1 us; the launch traced here: 27 us
  Pallas kernels  26.3 us (97%)
  between operations  0.64 us (2%)
    pallas_call x1, Pallas kernels, body(): pl.pallas_call(functools.partial(exchange_kernel, sizes, metal_map.shape)...  24.3 us
    pallas_call x1, Pallas kernels, body(): pl.pallas_call(functools.partial(finish_kernel, cell_count), out_shape=[j...  1.98 us

profile of v7, /device:TPU:1, one launch (start us, length us, event | category | flops | bytes accessed | tf_op | source)
XLA Modules:
  0.0 27.0 jit_solution(3066303238214498391)
XLA Ops:
  0.6 24.3 %shard_map.102 = (f32[4,6,16,16,128]{4,3,2,1,0:T(8,128)S(1)}, f32[16,128]{1,0:T(8,128)S(1)}, f32[2,4,3,8,8,128]{5,4,3,2,1,0:T(8,128)S(1)}, f32[24,128]{1,0:T(8,128)S(1)}, f32[7,256,128]{2,1,0:T(8,128)S(1)}) custom-call(f32[3,256,128]{2,1,0:T(8,128)} %bitcast.3, f32[3,256,128]{2,1,0:T(8,128)} %bitcast.4, f32[256,128]{1,0:T(8,128)} %bitcast.5, ...), custom_call_target="tpu_custom_call" | custom-call | tf_op jit(solution)/shard_map/pallas_call | solution.py:721
  25.0 2.0 %shard_map.103 = (f32[3,16,16,128]{3,2,1,0:T(8,128)}, f32[3,16,16,128]{3,2,1,0:T(8,128)}, f32[2,2,6,3,8,8,128]{6,5,4,3,2,1,0:T(8,128)}, f32[4,3]{1,0:T(4,128)}) custom-call(f32[7,256,128]{2,1,0:T(8,128)S(1)} %get-tuple-element.9.k0, f32[4,6,16,16,128]{4,3,2,1,0:T(8,128)S(1)} %get-tuple-element.10.own, f32[16,128]{1,0:T(8,128)S(1)} %get-tuple-element.11.gram, ...), custom_call_target="tpu_custom_call" | custom-call | tf_op jit(solution)/shard_map/pallas_call | solution.py:764

commit v8 on v7

--- a/solution.py
+++ b/solution.py
@@ -421,6 +421,9 @@
     interior(2, EDGE + 1, EDGE + OWN - 1, 0)
     interior(3, EDGE + 2, EDGE + OWN - 1, 1)
     interior(4, EDGE + 2, EDGE + OWN - 2, 0)
+    keep(interior_products(0, none), place < 6, False)
+    keep(interior_products(8, none), place >= 2, True)
+    acc_rows[pl.ds(8 * len(PAIRS), 8), :] = zero
     pl.semaphore_wait(heard.at[2], len(beside[2:]))
     for number, (side_x, side_y) in enumerate(corners):
         rows = pl.ds(0, 8 if side_x == side_y else CORNER_ROWS)
@@ -432,9 +435,6 @@
     pl.semaphore_wait(heard.at[0], len(near))
     for axis, step in far:
         signal(heard.at[1], along(axis, step))
-    keep(interior_products(0, none), place < 6, False)
-    keep(interior_products(8, none), place >= 2, True)
-    acc_rows[pl.ds(8 * len(PAIRS), 8), :] = zero
 
     for copy in copies[2:4]:
         copy.wait_recv()

time: 27.1 us -> 27.4 us (1.011)
  Pallas kernels: 26.3 us -> 26.7 us
    pallas_call x1, Pallas kernels: 24.3 us -> 24.7 us  [body(): pl.pallas_call(functools.partial(exchange_kernel, sizes, metal_map.shape)...]
where the time goes in v8:
time: 27.4 us; the launch traced here: 27.3 us
  Pallas kernels  26.7 us (97%)
  between operations  0.64 us (2%)
    pallas_call x1, Pallas kernels, body(): pl.pallas_call(functools.partial(exchange_kernel, sizes, metal_map.shape)...  24.7 us
    pallas_call x1, Pallas kernels, body(): pl.pallas_call(functools.partial(finish_kernel, cell_count), out_shape=[j...  1.98 us

profile of v8, /device:TPU:1, one launch (start us, length us, event | category | flops | bytes accessed | tf_op | source)
XLA Modules:
  0.0 27.3 jit_solution(917260713362391330)
XLA Ops:
  0.6 24.7 %shard_map.102 = (f32[4,6,16,16,128]{4,3,2,1,0:T(8,128)S(1)}, f32[16,128]{1,0:T(8,128)S(1)}, f32[2,4,3,8,8,128]{5,4,3,2,1,0:T(8,128)S(1)}, f32[24,128]{1,0:T(8,128)S(1)}, f32[7,256,128]{2,1,0:T(8,128)S(1)}) custom-call(f32[3,256,128]{2,1,0:T(8,128)} %bitcast.3, f32[3,256,128]{2,1,0:T(8,128)} %bitcast.4, f32[256,128]{1,0:T(8,128)} %bitcast.5, ...), custom_call_target="tpu_custom_call" | custom-call | tf_op jit(solution)/shard_map/pallas_call | solution.py:721
  25.3 2.0 %shard_map.103 = (f32[3,16,16,128]{3,2,1,0:T(8,128)}, f32[3,16,16,128]{3,2,1,0:T(8,128)}, f32[2,2,6,3,8,8,128]{6,5,4,3,2,1,0:T(8,128)}, f32[4,3]{1,0:T(4,128)}) custom-call(f32[7,256,128]{2,1,0:T(8,128)S(1)} %get-tuple-element.9.k0, f32[4,6,16,16,128]{4,3,2,1,0:T(8,128)S(1)} %get-tuple-element.10.own, f32[16,128]{1,0:T(8,128)S(1)} %get-tuple-element.11.gram, ...), custom_call_target="tpu_custom_call" | custom-call | tf_op jit(solution)/shard_map/pallas_call | solution.py:764

commit v9 on v7

--- a/solution.py
+++ b/solution.py
@@ -662,11 +662,11 @@
         return jnp.broadcast_to(table[pl.ds(number, 1), :], (8, 128))
 
     def pole_part(i):
-        return (i // 3, pl.ds(0, 2), pl.ds(0, POLES), i % 3)
+        return (i // 6, pl.ds(0, 2), pl.ds(0, POLES), i // 2 % 3, pl.ds(i % 2 * 4, 4))
 
     def pole_cells(i, carry):
-        slot, c = i // 3, i % 3
-        for x in range(8):
+        slot, c = i // 6, i // 2 % 3
+        for x in [i % 2 * 4 + k for k in range(4)]:
             field = [tiles[slot, j, c, x] for j in range(STEPS)]
             for p in range(POLES):
                 poles[slot, 1, p, c, x] = functools.reduce(
@@ -680,7 +680,7 @@
         ).start()
         return carry
 
-    lax.fori_loop(0, 3 * MS, pole_cells, 0)
+    lax.fori_loop(0, 6 * MS, pole_cells, 0)
 
     for half, out in enumerate((out_e, out_h)):
 
@@ -696,7 +696,7 @@
 
         lax.fori_loop(0, OWN // 4, field_cells, 0)
         store(fields.at[pl.ds(3 * half, 3)], out)
-    for i in range(3 * MS):
+    for i in range(6 * MS):
         pltpu.make_async_copy(poles.at[pole_part(i)], out_poles.at[pole_part(i)], pole_sem.at[i]).wait()
     for copy in stores:
         copy.wait()
@@ -776,7 +776,7 @@
             pltpu.VMEM((56, depth), f32),
             pltpu.VMEM((6, OWN, OWN, depth), f32),
             pltpu.VMEM((MS, 2, POLES, 3, 8, 8, depth), f32),
-            dma((3 * MS,)),
+            dma((6 * MS,)),
             dma((3,)),
         ],
         compiler_params=pltpu.CompilerParams(vmem_limit_bytes=VMEM_LIMIT),

time: 27.1 us -> 27.2 us (level)
  no operation moved by 1% of the time
where the time goes in v9:
time: 27.2 us; the launch traced here: 27.1 us
  Pallas kernels  26.4 us (97%)
  between operations  0.64 us (2%)
    pallas_call x1, Pallas kernels, body(): pl.pallas_call(functools.partial(exchange_kernel, sizes, metal_map.shape)...  24.3 us
    pallas_call x1, Pallas kernels, body(): pl.pallas_call(functools.partial(finish_kernel, cell_count), out_shape=[j...  2.08 us

profile of v9, /device:TPU:1, one launch (start us, length us, event | category | flops | bytes accessed | tf_op | source)
XLA Modules:
  0.0 27.1 jit_solution(11985091497940257966)
XLA Ops:
  0.6 24.3 %shard_map.102 = (f32[4,6,16,16,128]{4,3,2,1,0:T(8,128)S(1)}, f32[16,128]{1,0:T(8,128)S(1)}, f32[2,4,3,8,8,128]{5,4,3,2,1,0:T(8,128)S(1)}, f32[24,128]{1,0:T(8,128)S(1)}, f32[7,256,128]{2,1,0:T(8,128)S(1)}) custom-call(f32[3,256,128]{2,1,0:T(8,128)} %bitcast.3, f32[3,256,128]{2,1,0:T(8,128)} %bitcast.4, f32[256,128]{1,0:T(8,128)} %bitcast.5, ...), custom_call_target="tpu_custom_call" | custom-call | tf_op jit(solution)/shard_map/pallas_call | solution.py:721
  25.0 2.1 %shard_map.103 = (f32[3,16,16,128]{3,2,1,0:T(8,128)}, f32[3,16,16,128]{3,2,1,0:T(8,128)}, f32[2,2,6,3,8,8,128]{6,5,4,3,2,1,0:T(8,128)}, f32[4,3]{1,0:T(4,128)}) custom-call(f32[7,256,128]{2,1,0:T(8,128)S(1)} %get-tuple-element.9.k0, f32[4,6,16,16,128]{4,3,2,1,0:T(8,128)S(1)} %get-tuple-element.10.own, f32[16,128]{1,0:T(8,128)S(1)} %get-tuple-element.11.gram, ...), custom_call_target="tpu_custom_call" | custom-call | tf_op jit(solution)/shard_map/pallas_call | solution.py:764
